TPU v7x, 256 devices: a whole 4x4x8 slice. The times are simulated.
256 devices in a mesh: section: 4 (over x), replica: 64 (over z, y, core).
Axes of the slice: x: 4, y: 4, z: 8, core: 2. Of those that a mesh axis runs over, the one named last changes fastest.
Arguments:
- tokens: bfloat16 [4, 64, 2560], P(None, 'replica'), may hold values from -6 to 6
- cotangent: bfloat16 [4, 64, 2560], P(None, 'replica'), may hold values from -6 to 6
- wiring: int32 [4, 4, 1], replicated, may hold values from 0 to 3; in each aligned block of 4 rows (0 to 3, 4 to 7, ..., all dimensions but the last counted through in order) at most 2 rows name the same one
- lengths: int32 [4], replicated, may hold values from 16 to 64, as said below
- in_proj: bfloat16 [4, 64, 2560, 640], P('section', 'replica'), may hold values from -0.125 to 0.125
- out_proj: bfloat16 [4, 64, 2560, 640], P('section', 'replica'), may hold values from -0.0625 to 0.0625
- section_gain: bfloat16 [4, 4, 2560], P('section'), may hold values from 0.099609375 to 1.8984375
Outputs:
- input_grad: bfloat16 [4, 64, 2560], P('section', 'replica')
- in_grad: bfloat16 [4, 2560, 10240], P('section', None, 'replica')
- out_grad: bfloat16 [4, 2560, 10240], P('section', None, 'replica')
Inputs may be any that keep to these rules, and one draw needn't show every extreme that they name: wiring[t, i, 0] is the replica of section t that processes micro-batch i; at every section no replica is named by more than 2 micro-batches, and at some section one is named by exactly 2. `lengths`: some micro-batch has exactly 64 live tokens and some exactly 16.
All inputs are finite; a program needn't handle non-finite values.
Results may differ from a plain program's by a relative error of at most 0.027.
Values may be sent and summed in bfloat16 or wider, within the bound.
A program may use at most 128 MiB of HBM per device.

v0:
```python
import jax
import jax.numpy as jnp
from jax import lax
from jax.sharding import PartitionSpec as P

GROUPS = 4
CAP = 2


gelu_coeff = 0.7978845608028654
gelu_cubic = 0.044715
epsilon = 1e-05


def swapped(block, axis, distance):
    count = lax.axis_size(axis)
    route = []
    for low in range(count):
        high = low | 1 << distance
        if high != low and high < count:
            route += [(low, high), (high, low)]
    return lax.ppermute(block, axis, route)


def from_behind(x, axis, by):
    peers = lax.axis_size(axis)
    pairs = [(i, i + by) for i in range(peers) if 0 <= i + by < peers]
    return lax.ppermute(x, axis, pairs)


def from_root(block, axis, holder):
    block = jnp.where(lax.axis_index(axis) == holder, block, jnp.zeros_like(block))
    return lax.psum(block, axis)


def bit_set(replica_pos, bit):
    return replica_pos // (1 << bit) % 2 == 1


def gather_pieces(block, bits, dim):
    replica_pos = lax.axis_index("replica")
    for bit in bits:
        other = swapped(block, "replica", bit)
        upper = bit_set(replica_pos, bit)
        first = jnp.where(upper, other, block)
        second = jnp.where(upper, block, other)
        block = jnp.concatenate([first, second], dim)
    return block


def reduce_pieces(block, bits, dim):
    replica_pos = lax.axis_index("replica")
    for bit in reversed(bits):
        half = block.shape[dim] // 2
        upper = bit_set(replica_pos, bit).astype(jnp.int32)
        keep = lax.dynamic_slice_in_dim(block, upper * half, half, axis=dim)
        sending = lax.dynamic_slice_in_dim(block, (1 - upper) * half, half, axis=dim)
        block = keep + swapped(sending.astype(jnp.bfloat16), "replica", bit).astype(sending.dtype)
    return block


def route_sum(block, bits):
    replica_pos = lax.axis_index("replica")
    for bit in reversed(bits):
        half = block.shape[0] // 2
        upper = bit_set(replica_pos, bit).astype(jnp.int32)
        keep = lax.dynamic_slice_in_dim(block, upper * half, half, axis=0)
        sending = lax.dynamic_slice_in_dim(block, (1 - upper) * half, half, axis=0)
        block = keep + swapped(sending, "replica", bit)
    return block[0]


def pass_section(block, offset):
    return from_behind(block, "section", offset)


def section_places(targets):
    ordinal = jnp.arange(targets.shape[0], dtype=jnp.int32)
    earlier = (targets[:, None] == targets[None, :]) & (ordinal[None, :] < ordinal[:, None])
    return targets * CAP + jnp.sum(earlier.astype(jnp.int32), axis=1)


def route_slots(buffer, source, destination, group, group_bits):
    slot_ids = jnp.arange(GROUPS * CAP, dtype=jnp.int32)
    own_slots = group * CAP + jnp.arange(CAP, dtype=jnp.int32)
    to_dest = (destination[None, :] == slot_ids[:, None]).astype(jnp.float32)
    from_own = (source[:, None] == own_slots[None, :]).astype(jnp.float32)
    select = jnp.dot(to_dest, from_own).astype(jnp.bfloat16)
    sending = jnp.einsum("dc,cpf->dpf", select, buffer, preferred_element_type=jnp.float32).astype(
        jnp.bfloat16
    )
    return route_sum(sending.reshape((GROUPS, CAP) + buffer.shape[1:]), group_bits)


def home_in(local, destination, group, group_bits):
    slot_ids = jnp.arange(GROUPS * CAP, dtype=jnp.int32)
    to_dest = (destination[None, :] == slot_ids[:, None]).astype(jnp.bfloat16)
    gathered = jnp.einsum("di,iqf->dqf", to_dest, local, preferred_element_type=jnp.float32).astype(
        jnp.bfloat16
    )
    chosen = (jnp.arange(GROUPS, dtype=jnp.int32) == group)[None, :, None, None]
    placed = jnp.where(chosen, gathered[:, None], jnp.zeros((), jnp.bfloat16))
    sub_rows = local.shape[1]
    feature = local.shape[2]
    return route_sum(placed.reshape(GROUPS, CAP, GROUPS * sub_rows, feature), group_bits)


def home_out(slots, here, group, group_bits):
    own_slots = group * CAP + jnp.arange(CAP, dtype=jnp.int32)
    from_own = (here[:, None] == own_slots[None, :]).astype(jnp.bfloat16)
    cap_count, piece_rows, feature = slots.shape
    split_rows = slots.reshape(cap_count, GROUPS, piece_rows // GROUPS, feature)
    spread = jnp.einsum(
        "ic,cgqf->giqf", from_own, split_rows, preferred_element_type=jnp.float32
    ).astype(jnp.bfloat16)
    return route_sum(spread, group_bits)


def norm_rows(rows, gain_vec):
    flattened = rows.astype(jnp.float32)
    inv_rms = lax.rsqrt(jnp.mean(flattened * flattened, axis=-1, keepdims=True) + epsilon)
    normed = (flattened * inv_rms * gain_vec.astype(jnp.float32)).astype(jnp.bfloat16)
    return (flattened, inv_rms, normed)


def forward_hop(entered, live, w_in, w_out, gain_vec, piece_bits):
    flattened, inv_rms, normed = norm_rows(entered, gain_vec)
    full_rows = gather_pieces(normed[None], piece_bits, 2)[0]
    cap_count, tok_count, feature = full_rows.shape
    pre_act = jnp.dot(full_rows.reshape(-1, feature), w_in, preferred_element_type=jnp.float32)
    activated = jax.nn.gelu(pre_act, approximate=True).astype(jnp.bfloat16)
    partial_value = lax.dot_general(
        activated, w_out, (((1,), (1,)), ((), ())), preferred_element_type=jnp.float32
    )
    branch = reduce_pieces(partial_value.reshape(cap_count, tok_count, feature), piece_bits, 1)
    return (flattened + live[..., None] * branch).astype(jnp.bfloat16)


def backward_hop(stored, upstream, live, w_in, w_out, gain_vec, piece_bits):
    flattened, inv_rms, normed = norm_rows(stored, gain_vec)
    masked = (upstream.astype(jnp.float32) * live[..., None]).astype(jnp.bfloat16)
    both = gather_pieces(jnp.stack([normed, masked]), piece_bits, 2)
    cap_count, tok_count, feature = both.shape[1:]
    normed_all = both[0].reshape(-1, feature)
    masked_all = both[1].reshape(-1, feature)
    pre_act = jnp.dot(normed_all, w_in, preferred_element_type=jnp.float32)
    activated = jax.nn.gelu(pre_act, approximate=True).astype(jnp.bfloat16)
    act_grad = jnp.dot(masked_all, w_out, preferred_element_type=jnp.float32)
    inner_arg = gelu_coeff * (pre_act + gelu_cubic * pre_act * pre_act * pre_act)
    tangent = jnp.tanh(inner_arg)
    derivative = 0.5 * (1.0 + tangent) + 0.5 * pre_act * (1.0 - tangent * tangent) * gelu_coeff * (
        1.0 + 3.0 * gelu_cubic * pre_act * pre_act
    )
    pre_grad = (act_grad * derivative).astype(jnp.bfloat16)
    partial_value = lax.dot_general(
        pre_grad, w_in, (((1,), (1,)), ((), ())), preferred_element_type=jnp.float32
    )
    norm_grad = reduce_pieces(partial_value.reshape(cap_count, tok_count, feature), piece_bits, 1)
    pulled = norm_grad * gain_vec.astype(jnp.float32)
    hidden_grad = (
        upstream.astype(jnp.float32)
        + inv_rms * pulled
        - flattened
        * inv_rms
        * inv_rms
        * inv_rms
        * jnp.mean(flattened * pulled, axis=-1, keepdims=True)
    )
    return (hidden_grad.astype(jnp.bfloat16), (normed_all, masked_all, activated, pre_grad))


def body(tokens, cotangent, wiring, lengths, in_proj, out_proj, section_gain):
    section_count = lax.axis_size("section")
    replica_count = lax.axis_size("replica")
    section_idx = lax.axis_index("section")
    replica_pos = lax.axis_index("replica")
    group = replica_pos % GROUPS
    piece = replica_pos // GROUPS
    low_count = GROUPS.bit_length() - 1
    all_count = replica_count.bit_length() - 1
    group_bits = list(range(low_count))
    piece_bits = list(range(low_count, all_count))
    token_count = tokens.shape[1] * replica_count
    piece_rows = token_count // (replica_count // GROUPS)
    w_in = in_proj[0, 0]
    w_out = out_proj[0, 0]
    gain_vec = lax.dynamic_index_in_dim(section_gain[0], group, 0, keepdims=False)
    all_places = jax.vmap(section_places)(wiring[:, :, 0])
    here = lax.dynamic_index_in_dim(all_places, section_idx, 0, keepdims=False)
    before = lax.dynamic_index_in_dim(
        all_places, jnp.maximum(section_idx - 1, 0), 0, keepdims=False
    )
    own_slots = group * CAP + jnp.arange(CAP, dtype=jnp.int32)
    slot_length = jnp.sum(
        jnp.where(here[:, None] == own_slots[None, :], lengths[:, None], 0), axis=0
    )
    row_ids = piece * piece_rows + jnp.arange(piece_rows, dtype=jnp.int32)
    live = (row_ids[None, :] < slot_length[:, None]).astype(jnp.float32)
    entered = home_in(tokens, here, group, group_bits)
    stored = entered
    current = entered
    for hop_index in range(section_count):
        if hop_index > 0:
            entered = route_slots(current, before, here, group, group_bits)
            stored = jnp.where(section_idx == hop_index, entered, stored)
        if hop_index + 1 < section_count:
            leaving = forward_hop(entered, live, w_in, w_out, gain_vec, piece_bits)
            current = pass_section(leaving, 1)
    upstream = home_in(cotangent, here, group, group_bits)
    saved = None
    final_grad = upstream
    for back_index in range(section_count):
        owner = section_idx == section_count - 1 - back_index
        hidden_grad, fresh = backward_hop(stored, upstream, live, w_in, w_out, gain_vec, piece_bits)
        if saved is None:
            saved = fresh
        else:
            saved = jax.tree.map(
                lambda new_value, old_value: jnp.where(owner, new_value, old_value), fresh, saved
            )
        if back_index + 1 < section_count:
            upstream = pass_section(route_slots(hidden_grad, here, before, group, group_bits), -1)
        else:
            final_grad = hidden_grad
    normed_all, masked_all, activated, pre_grad = saved
    homeward = home_out(final_grad, here, group, group_bits)
    shared = from_root(homeward, "section", 0)
    per_section = shared.shape[0] // section_count
    input_grad = lax.dynamic_slice_in_dim(shared, section_idx * per_section, per_section, 0)
    in_local = lax.dot_general(
        normed_all, pre_grad, (((0,), (0,)), ((), ())), preferred_element_type=jnp.float32
    )
    in_part = reduce_pieces(in_local, group_bits, 1)
    out_local = lax.dot_general(
        masked_all, activated, (((0,), (0,)), ((), ())), preferred_element_type=jnp.float32
    )
    out_part = reduce_pieces(out_local, group_bits, 1)
    return (input_grad, in_part.astype(jnp.bfloat16)[None], out_part.astype(jnp.bfloat16)[None])


def solution(mesh):
    in_specs = (
        P(None, "replica", None),
        P(None, "replica", None),
        P(),
        P(),
        P("section", "replica", None, None),
        P("section", "replica", None, None),
        P("section", None, None),
    )
    out_specs = (
        P("section", "replica", None),
        P("section", None, "replica"),
        P("section", None, "replica"),
    )
    return jax.shard_map(body, mesh=mesh, in_specs=in_specs, out_specs=out_specs, check_vma=False)
```

profile of v0, /device:TPU:1, one launch (start us, length us, event | category | flops | bytes accessed | tf_op | source)
XLA Modules:
  0.0 796.4 jit_solution(9608869330052498902)
XLA Ops:
  27.8 8.1 %collective-permute-done.6 = bf16[1,2,16,2560]{3,2,1,0:T(8,128)(2,1)} collective-permute-done((bf16[1,2,16,2560]{3,2,1,0:T(8,128)(2,1)}, bf16[1,2,16,2560]{3,2,1,0:T(8,128)(2,1)}, u32[]{:S(2)}, u32[]{:S(2)}) %collective-permute-start.6) | collective-permute-done | bytes 163872 | tf_op jit(solution)/shard_map/ppermute | solution.py:22
  43.6 15.5 %collective-permute-done.7 = bf16[1,2,32,2560]{3,2,1,0:T(8,128)(2,1)} collective-permute-done((bf16[1,2,32,2560]{3,2,1,0:T(8,128)(2,1)}, bf16[1,2,32,2560]{3,2,1,0:T(8,128)(2,1)}, u32[]{:S(2)}, u32[]{:S(2)}) %collective-permute-start.7) | collective-permute-done | bytes 327712 | tf_op jit(solution)/shard_map/ppermute | solution.py:22
  67.3 10.6 %collective-permute-done.8 = bf16[2,32,2560]{2,1,0:T(8,128)(2,1)} collective-permute-done((bf16[2,32,2560]{2,1,0:T(8,128)(2,1)}, bf16[2,32,2560]{2,1,0:T(8,128)(2,1)}, u32[]{:S(2)}, u32[]{:S(2)}) %collective-permute-start.8) | collective-permute-done | bytes 327712 | tf_op jit(solution)/shard_map/ppermute | solution.py:22
  80.3 10.4 %collective-permute-done.9 = bf16[2,16,2560]{2,1,0:T(8,128)(2,1)} collective-permute-done((bf16[2,16,2560]{2,1,0:T(8,128)(2,1)S(1)}, bf16[2,16,2560]{2,1,0:T(8,128)(2,1)}, u32[]{:S(2)}, u32[]{:S(2)}) %collective-permute-start.9) | collective-permute-done | bytes 163872 | tf_op jit(solution)/shard_map/ppermute | solution.py:22
  122.7 8.9 %collective-permute-done.17 = bf16[1,2,16,2560]{3,2,1,0:T(8,128)(2,1)S(1)} collective-permute-done((bf16[1,2,16,2560]{3,2,1,0:T(8,128)(2,1)S(1)}, bf16[1,2,16,2560]{3,2,1,0:T(8,128)(2,1)S(1)}, u32[]{:S(2)}, u32[]{:S(2)}) %collective-permute-start.17) | collective-permute-done | bytes 163872 | tf_op jit(solution)/shard_map/ppermute | solution.py:22
  133.8 17.3 %collective-permute-done.18 = bf16[1,2,32,2560]{3,2,1,0:T(8,128)(2,1)S(1)} collective-permute-done((bf16[1,2,32,2560]{3,2,1,0:T(8,128)(2,1)S(1)}, bf16[1,2,32,2560]{3,2,1,0:T(8,128)(2,1)S(1)}, u32[]{:S(2)}, u32[]{:S(2)}) %collective-permute-start.18) | collective-permute-done | bytes 327712 | tf_op jit(solution)/shard_map/ppermute | solution.py:22
  157.4 9.7 %collective-permute-done.19 = bf16[2,32,2560]{2,1,0:T(8,128)(2,1)S(1)} collective-permute-done((bf16[2,32,2560]{2,1,0:T(8,128)(2,1)S(1)}, bf16[2,32,2560]{2,1,0:T(8,128)(2,1)S(1)}, u32[]{:S(2)}, u32[]{:S(2)}) %collective-permute-start.19) | collective-permute-done | bytes 327712 | tf_op jit(solution)/shard_map/ppermute | solution.py:22
  167.3 9.1 %collective-permute-done.20 = bf16[2,16,2560]{2,1,0:T(8,128)(2,1)S(1)} collective-permute-done((bf16[2,16,2560]{2,1,0:T(8,128)(2,1)S(1)}, bf16[2,16,2560]{2,1,0:T(8,128)(2,1)S(1)}, u32[]{:S(2)}, u32[]{:S(2)}) %collective-permute-start.20) | collective-permute-done | bytes 163872 | tf_op jit(solution)/shard_map/ppermute | solution.py:22
  208.7 8.2 %collective-permute-done.28 = bf16[1,2,16,2560]{3,2,1,0:T(8,128)(2,1)S(1)} collective-permute-done((bf16[1,2,16,2560]{3,2,1,0:T(8,128)(2,1)S(1)}, bf16[1,2,16,2560]{3,2,1,0:T(8,128)(2,1)S(1)}, u32[]{:S(2)}, u32[]{:S(2)}) %collective-permute-start.28) | collective-permute-done | bytes 163872 | tf_op jit(solution)/shard_map/ppermute | solution.py:22
  219.0 17.1 %collective-permute-done.29 = bf16[1,2,32,2560]{3,2,1,0:T(8,128)(2,1)S(1)} collective-permute-done((bf16[1,2,32,2560]{3,2,1,0:T(8,128)(2,1)S(1)}, bf16[1,2,32,2560]{3,2,1,0:T(8,128)(2,1)S(1)}, u32[]{:S(2)}, u32[]{:S(2)}) %collective-permute-start.29) | collective-permute-done | bytes 327712 | tf_op jit(solution)/shard_map/ppermute | solution.py:22
  241.3 12.0 %collective-permute-done.30 = bf16[2,32,2560]{2,1,0:T(8,128)(2,1)S(1)} collective-permute-done((bf16[2,32,2560]{2,1,0:T(8,128)(2,1)S(1)}, bf16[2,32,2560]{2,1,0:T(8,128)(2,1)S(1)}, u32[]{:S(2)}, u32[]{:S(2)}) %collective-permute-start.30) | collective-permute-done | bytes 327712 | tf_op jit(solution)/shard_map/ppermute | solution.py:22
  253.5 10.1 %collective-permute-done.31 = bf16[2,16,2560]{2,1,0:T(8,128)(2,1)S(1)} collective-permute-done((bf16[2,16,2560]{2,1,0:T(8,128)(2,1)S(1)}, bf16[2,16,2560]{2,1,0:T(8,128)(2,1)S(1)}, u32[]{:S(2)}, u32[]{:S(2)}) %collective-permute-start.31) | collective-permute-done | bytes 163872 | tf_op jit(solution)/shard_map/ppermute | solution.py:22
  299.0 17.1 %collective-permute-done.39 = bf16[2,2,16,2560]{3,2,1,0:T(8,128)(2,1)S(1)} collective-permute-done((bf16[2,2,16,2560]{3,2,1,0:T(8,128)(2,1)S(1)}, bf16[2,2,16,2560]{3,2,1,0:T(8,128)(2,1)S(1)}, u32[]{:S(2)}, u32[]{:S(2)}) %collective-permute-start.39) | collective-permute-done | bytes 327712 | tf_op jit(solution)/shard_map/ppermute | solution.py:22
  318.1 31.6 %collective-permute-done.40 = bf16[2,2,32,2560]{3,2,1,0:T(8,128)(2,1)S(1)} collective-permute-done((bf16[2,2,32,2560]{3,2,1,0:T(8,128)(2,1)S(1)}, bf16[2,2,32,2560]{3,2,1,0:T(8,128)(2,1)S(1)}, u32[]{:S(2)}, u32[]{:S(2)}) %collective-permute-start.40) | collective-permute-done | bytes 655392 | tf_op jit(solution)/shard_map/ppermute | solution.py:22
  356.9 10.3 %collective-permute-done.41 = bf16[2,32,2560]{2,1,0:T(8,128)(2,1)S(1)} collective-permute-done((bf16[2,32,2560]{2,1,0:T(8,128)(2,1)S(1)}, bf16[2,32,2560]{2,1,0:T(8,128)(2,1)S(1)}, u32[]{:S(2)}, u32[]{:S(2)}) %collective-permute-start.41) | collective-permute-done | bytes 327712 | tf_op jit(solution)/shard_map/ppermute | solution.py:22
  367.5 9.3 %collective-permute-done.42 = bf16[2,16,2560]{2,1,0:T(8,128)(2,1)S(1)} collective-permute-done((bf16[2,16,2560]{2,1,0:T(8,128)(2,1)S(1)}, bf16[2,16,2560]{2,1,0:T(8,128)(2,1)S(1)}, u32[]{:S(2)}, u32[]{:S(2)}) %collective-permute-start.42) | collective-permute-done | bytes 163872 | tf_op jit(solution)/shard_map/ppermute | solution.py:22
  410.0 16.3 %collective-permute-done.50 = bf16[2,2,16,2560]{3,2,1,0:T(8,128)(2,1)S(1)} collective-permute-done((bf16[2,2,16,2560]{3,2,1,0:T(8,128)(2,1)S(1)}, bf16[2,2,16,2560]{3,2,1,0:T(8,128)(2,1)S(1)}, u32[]{:S(2)}, u32[]{:S(2)}) %collective-permute-start.50) | collective-permute-done | bytes 327712 | tf_op jit(solution)/shard_map/ppermute | solution.py:22
  428.1 31.6 %collective-permute-done.51 = bf16[2,2,32,2560]{3,2,1,0:T(8,128)(2,1)S(1)} collective-permute-done((bf16[2,2,32,2560]{3,2,1,0:T(8,128)(2,1)S(1)}, bf16[2,2,32,2560]{3,2,1,0:T(8,128)(2,1)S(1)}, u32[]{:S(2)}, u32[]{:S(2)}) %collective-permute-start.51) | collective-permute-done | bytes 655392 | tf_op jit(solution)/shard_map/ppermute | solution.py:22
  465.5 10.4 %collective-permute-done.52 = bf16[2,32,2560]{2,1,0:T(8,128)(2,1)S(1)} collective-permute-done((bf16[2,32,2560]{2,1,0:T(8,128)(2,1)S(1)}, bf16[2,32,2560]{2,1,0:T(8,128)(2,1)S(1)}, u32[]{:S(2)}, u32[]{:S(2)}) %collective-permute-start.52) | collective-permute-done | bytes 327712 | tf_op jit(solution)/shard_map/ppermute | solution.py:22
  476.1 10.2 %collective-permute-done.53 = bf16[2,16,2560]{2,1,0:T(8,128)(2,1)S(1)} collective-permute-done((bf16[2,16,2560]{2,1,0:T(8,128)(2,1)S(1)}, bf16[2,16,2560]{2,1,0:T(8,128)(2,1)S(1)}, u32[]{:S(2)}, u32[]{:S(2)}) %collective-permute-start.53) | collective-permute-done | bytes 163872 | tf_op jit(solution)/shard_map/ppermute | solution.py:22
  517.8 16.2 %collective-permute-done.61 = bf16[2,2,16,2560]{3,2,1,0:T(8,128)(2,1)S(1)} collective-permute-done((bf16[2,2,16,2560]{3,2,1,0:T(8,128)(2,1)S(1)}, bf16[2,2,16,2560]{3,2,1,0:T(8,128)(2,1)S(1)}, u32[]{:S(2)}, u32[]{:S(2)}) %collective-permute-start.61) | collective-permute-done | bytes 327712 | tf_op jit(solution)/shard_map/ppermute | solution.py:22
  537.0 31.6 %collective-permute-done.62 = bf16[2,2,32,2560]{3,2,1,0:T(8,128)(2,1)S(1)} collective-permute-done((bf16[2,2,32,2560]{3,2,1,0:T(8,128)(2,1)S(1)}, bf16[2,2,32,2560]{3,2,1,0:T(8,128)(2,1)S(1)}, u32[]{:S(2)}, u32[]{:S(2)}) %collective-permute-start.62) | collective-permute-done | bytes 655392 | tf_op jit(solution)/shard_map/ppermute | solution.py:22
  575.3 9.5 %collective-permute-done.63 = bf16[2,32,2560]{2,1,0:T(8,128)(2,1)S(1)} collective-permute-done((bf16[2,32,2560]{2,1,0:T(8,128)(2,1)S(1)}, bf16[2,32,2560]{2,1,0:T(8,128)(2,1)S(1)}, u32[]{:S(2)}, u32[]{:S(2)}) %collective-permute-start.63) | collective-permute-done | bytes 327712 | tf_op jit(solution)/shard_map/ppermute | solution.py:22
  585.0 9.8 %collective-permute-done.64 = bf16[2,16,2560]{2,1,0:T(8,128)(2,1)S(1)} collective-permute-done((bf16[2,16,2560]{2,1,0:T(8,128)(2,1)S(1)}, bf16[2,16,2560]{2,1,0:T(8,128)(2,1)S(1)}, u32[]{:S(2)}, u32[]{:S(2)}) %collective-permute-start.64) | collective-permute-done | bytes 163872 | tf_op jit(solution)/shard_map/ppermute | solution.py:22
  626.7 16.1 %collective-permute-done.72 = bf16[2,2,16,2560]{3,2,1,0:T(8,128)(2,1)S(1)} collective-permute-done((bf16[2,2,16,2560]{3,2,1,0:T(8,128)(2,1)S(1)}, bf16[2,2,16,2560]{3,2,1,0:T(8,128)(2,1)S(1)}, u32[]{:S(2)}, u32[]{:S(2)}) %collective-permute-start.72) | collective-permute-done | bytes 327712 | tf_op jit(solution)/shard_map/ppermute | solution.py:22
  646.5 30.8 %collective-permute-done.73 = bf16[2,2,32,2560]{3,2,1,0:T(8,128)(2,1)S(1)} collective-permute-done((bf16[2,2,32,2560]{3,2,1,0:T(8,128)(2,1)S(1)}, bf16[2,2,32,2560]{3,2,1,0:T(8,128)(2,1)S(1)}, u32[]{:S(2)}, u32[]{:S(2)}) %collective-permute-start.73) | collective-permute-done | bytes 655392 | tf_op jit(solution)/shard_map/ppermute | solution.py:22
  683.5 9.4 %collective-permute-done.74 = bf16[2,32,2560]{2,1,0:T(8,128)(2,1)S(1)} collective-permute-done((bf16[2,32,2560]{2,1,0:T(8,128)(2,1)S(1)}, bf16[2,32,2560]{2,1,0:T(8,128)(2,1)S(1)}, u32[]{:S(2)}, u32[]{:S(2)}) %collective-permute-start.74) | collective-permute-done | bytes 327712 | tf_op jit(solution)/shard_map/ppermute | solution.py:22
  694.7 10.6 %collective-permute-done.75 = bf16[2,16,2560]{2,1,0:T(8,128)(2,1)} collective-permute-done((bf16[2,16,2560]{2,1,0:T(8,128)(2,1)}, bf16[2,16,2560]{2,1,0:T(8,128)(2,1)}, u32[]{:S(2)}, u32[]{:S(2)}) %collective-permute-start.75) | collective-permute-done | bytes 163872 | tf_op jit(solution)/shard_map/ppermute | solution.py:22
  724.4 12.9 %psum.7 = bf16[4,1,2560]{2,0,1:T(4,128)(2,1)S(1)} all-reduce(bf16[4,1,2560]{2,0,1:T(4,128)(2,1)S(1)} %fusion.248), channel_id=1, replica_groups=mesh['section'=4,'replica'=64] {'section'}, use_global_device_ids=true, to_apply=%region_10.11 | all-reduce | flops 10240 | bytes 40960 | tf_op jit(solution)/shard_map/psum | solution.py:33
  737.3 15.3 %collective-permute-done.82 = bf16[2560,320]{0,1:T(8,128)(2,1)} collective-permute-done((bf16[2560,320]{0,1:T(8,128)(2,1)}, bf16[2560,320]{0,1:T(8,128)(2,1)}, u32[]{:S(2)}, u32[]{:S(2)}) %collective-permute-start.82) | collective-permute-done | bytes 1638432 | tf_op jit(solution)/shard_map/ppermute | solution.py:22
  755.6 6.7 collective-permute-start.83
  762.3 25.4 %collective-permute-done.80 = bf16[2560,320]{0,1:T(8,128)(2,1)} collective-permute-done((bf16[2560,320]{0,1:T(8,128)(2,1)}, bf16[2560,320]{0,1:T(8,128)(2,1)}, u32[]{:S(2)}, u32[]{:S(2)}) %collective-permute-start.80) | collective-permute-done | bytes 1638432 | tf_op jit(solution)/shard_map/ppermute | solution.py:22
  (451 shorter events, 325.6 us)
Async XLA Ops:
  26.4 9.5 %collective-permute-start.6 = (bf16[1,2,16,2560]{3,2,1,0:T(8,128)(2,1)}, bf16[1,2,16,2560]{3,2,1,0:T(8,128)(2,1)}, u32[]{:S(2)}, u32[]{:S(2)}) collective-permute-start(bf16[1,2,16,2560]{3,2,1,0:T(8,128)(2,1)} %pad_maximum_fusion.18), channel_id=1, source_target_pairs={{0,16},{16,0},{1,17},{17,1},{2,18},{18,2},{3,19},{19,3},{4,20},{20... | collective-permute-start | bytes 491528 | tf_op jit(solution)/shard_map/ppermute | solution.py:22
  38.4 20.6 %collective-permute-start.7 = (bf16[1,2,32,2560]{3,2,1,0:T(8,128)(2,1)}, bf16[1,2,32,2560]{3,2,1,0:T(8,128)(2,1)}, u32[]{:S(2)}, u32[]{:S(2)}) collective-permute-start(bf16[1,2,32,2560]{3,2,1,0:T(8,128)(2,1)} %pad_maximum_fusion.11), channel_id=1, source_target_pairs={{0,32},{32,0},{1,33},{33,1},{2,34},{34,2},{3,35},{35,3},{4,36},{36... | collective-permute-start | bytes 983048 | tf_op jit(solution)/shard_map/ppermute | solution.py:22
  65.2 12.7 %collective-permute-start.8 = (bf16[2,32,2560]{2,1,0:T(8,128)(2,1)}, bf16[2,32,2560]{2,1,0:T(8,128)(2,1)}, u32[]{:S(2)}, u32[]{:S(2)}) collective-permute-start(bf16[2,32,2560]{2,1,0:T(8,128)(2,1)} %dynamic-slice_convert_fusion.10), channel_id=1, source_target_pairs={{0,32},{32,0},{1,33},{33,1},{2,34},{34,2},{3,35},{35,3},{4,36},{36... | collective-permute-start | bytes 983048 | tf_op jit(solution)/shard_map/ppermute | solution.py:22
  80.0 10.7 %collective-permute-start.9 = (bf16[2,16,2560]{2,1,0:T(8,128)(2,1)S(1)}, bf16[2,16,2560]{2,1,0:T(8,128)(2,1)}, u32[]{:S(2)}, u32[]{:S(2)}) collective-permute-start(bf16[2,16,2560]{2,1,0:T(8,128)(2,1)S(1)} %dynamic-slice_convert_fusion.17), channel_id=1, source_target_pairs={{0,16},{16,0},{1,17},{17,1},{2,18},{18,2},{3,19},{19,3},{4,20},{20... | collective-permute-start | bytes 491528 | tf_op jit(solution)/shard_map/ppermute | solution.py:22
  122.0 9.7 %collective-permute-start.17 = (bf16[1,2,16,2560]{3,2,1,0:T(8,128)(2,1)S(1)}, bf16[1,2,16,2560]{3,2,1,0:T(8,128)(2,1)S(1)}, u32[]{:S(2)}, u32[]{:S(2)}) collective-permute-start(bf16[1,2,16,2560]{3,2,1,0:T(8,128)(2,1)S(1)} %pad_maximum_fusion.19), channel_id=1, source_target_pairs={{0,16},{16,0},{1,17},{17,1},{2,18},{18,2},{3,19},{19,3},{4,20},{20... | collective-permute-start | bytes 491528 | tf_op jit(solution)/shard_map/ppermute | solution.py:22
  131.7 19.4 %collective-permute-start.18 = (bf16[1,2,32,2560]{3,2,1,0:T(8,128)(2,1)S(1)}, bf16[1,2,32,2560]{3,2,1,0:T(8,128)(2,1)S(1)}, u32[]{:S(2)}, u32[]{:S(2)}) collective-permute-start(bf16[1,2,32,2560]{3,2,1,0:T(8,128)(2,1)S(1)} %pad_maximum_fusion.12), channel_id=1, source_target_pairs={{0,32},{32,0},{1,33},{33,1},{2,34},{34,2},{3,35},{35,3},{4,36},{36... | collective-permute-start | bytes 983048 | tf_op jit(solution)/shard_map/ppermute | solution.py:22
  154.4 12.7 %collective-permute-start.19 = (bf16[2,32,2560]{2,1,0:T(8,128)(2,1)S(1)}, bf16[2,32,2560]{2,1,0:T(8,128)(2,1)S(1)}, u32[]{:S(2)}, u32[]{:S(2)}) collective-permute-start(bf16[2,32,2560]{2,1,0:T(8,128)(2,1)S(1)} %dynamic-slice_convert_fusion.9), channel_id=1, source_target_pairs={{0,32},{32,0},{1,33},{33,1},{2,34},{34,2},{3,35},{35,3},{4,36},{36... | collective-permute-start | bytes 983048 | tf_op jit(solution)/shard_map/ppermute | solution.py:22
  167.2 9.2 %collective-permute-start.20 = (bf16[2,16,2560]{2,1,0:T(8,128)(2,1)S(1)}, bf16[2,16,2560]{2,1,0:T(8,128)(2,1)S(1)}, u32[]{:S(2)}, u32[]{:S(2)}) collective-permute-start(bf16[2,16,2560]{2,1,0:T(8,128)(2,1)S(1)} %dynamic-slice_convert_fusion.16), channel_id=1, source_target_pairs={{0,16},{16,0},{1,17},{17,1},{2,18},{18,2},{3,19},{19,3},{4,20},{20... | collective-permute-start | bytes 491528 | tf_op jit(solution)/shard_map/ppermute | solution.py:22
  207.4 9.5 %collective-permute-start.28 = (bf16[1,2,16,2560]{3,2,1,0:T(8,128)(2,1)S(1)}, bf16[1,2,16,2560]{3,2,1,0:T(8,128)(2,1)S(1)}, u32[]{:S(2)}, u32[]{:S(2)}) collective-permute-start(bf16[1,2,16,2560]{3,2,1,0:T(8,128)(2,1)S(1)} %pad_maximum_fusion.20), channel_id=1, source_target_pairs={{0,16},{16,0},{1,17},{17,1},{2,18},{18,2},{3,19},{19,3},{4,20},{20... | collective-permute-start | bytes 491528 | tf_op jit(solution)/shard_map/ppermute | solution.py:22
  217.0 19.1 %collective-permute-start.29 = (bf16[1,2,32,2560]{3,2,1,0:T(8,128)(2,1)S(1)}, bf16[1,2,32,2560]{3,2,1,0:T(8,128)(2,1)S(1)}, u32[]{:S(2)}, u32[]{:S(2)}) collective-permute-start(bf16[1,2,32,2560]{3,2,1,0:T(8,128)(2,1)S(1)} %pad_maximum_fusion.13), channel_id=1, source_target_pairs={{0,32},{32,0},{1,33},{33,1},{2,34},{34,2},{3,35},{35,3},{4,36},{36... | collective-permute-start | bytes 983048 | tf_op jit(solution)/shard_map/ppermute | solution.py:22
  238.2 15.1 %collective-permute-start.30 = (bf16[2,32,2560]{2,1,0:T(8,128)(2,1)S(1)}, bf16[2,32,2560]{2,1,0:T(8,128)(2,1)S(1)}, u32[]{:S(2)}, u32[]{:S(2)}) collective-permute-start(bf16[2,32,2560]{2,1,0:T(8,128)(2,1)S(1)} %dynamic-slice_convert_fusion.8), channel_id=1, source_target_pairs={{0,32},{32,0},{1,33},{33,1},{2,34},{34,2},{3,35},{35,3},{4,36},{36... | collective-permute-start | bytes 983048 | tf_op jit(solution)/shard_map/ppermute | solution.py:22
  253.4 10.2 %collective-permute-start.31 = (bf16[2,16,2560]{2,1,0:T(8,128)(2,1)S(1)}, bf16[2,16,2560]{2,1,0:T(8,128)(2,1)S(1)}, u32[]{:S(2)}, u32[]{:S(2)}) collective-permute-start(bf16[2,16,2560]{2,1,0:T(8,128)(2,1)S(1)} %dynamic-slice_convert_fusion.15), channel_id=1, source_target_pairs={{0,16},{16,0},{1,17},{17,1},{2,18},{18,2},{3,19},{19,3},{4,20},{20... | collective-permute-start | bytes 491528 | tf_op jit(solution)/shard_map/ppermute | solution.py:22
  279.8 7.4 collective-permute-start.1
  298.5 17.6 %collective-permute-start.39 = (bf16[2,2,16,2560]{3,2,1,0:T(8,128)(2,1)S(1)}, bf16[2,2,16,2560]{3,2,1,0:T(8,128)(2,1)S(1)}, u32[]{:S(2)}, u32[]{:S(2)}) collective-permute-start(bf16[2,2,16,2560]{3,2,1,0:T(8,128)(2,1)S(1)} %pad_maximum_fusion.14), channel_id=1, source_target_pairs={{0,16},{16,0},{1,17},{17,1},{2,18},{18,2},{3,19},{19,3},{4,20},{20... | collective-permute-start | bytes 983048 | tf_op jit(solution)/shard_map/ppermute | solution.py:22
  316.3 33.3 %collective-permute-start.40 = (bf16[2,2,32,2560]{3,2,1,0:T(8,128)(2,1)S(1)}, bf16[2,2,32,2560]{3,2,1,0:T(8,128)(2,1)S(1)}, u32[]{:S(2)}, u32[]{:S(2)}) collective-permute-start(bf16[2,2,32,2560]{3,2,1,0:T(8,128)(2,1)S(1)} %pad_maximum_fusion.7), channel_id=1, source_target_pairs={{0,32},{32,0},{1,33},{33,1},{2,34},{34,2},{3,35},{35,3},{4,36},{36... | collective-permute-start | bytes 1966088 | tf_op jit(solution)/shard_map/ppermute | solution.py:22
  354.5 12.8 %collective-permute-start.41 = (bf16[2,32,2560]{2,1,0:T(8,128)(2,1)S(1)}, bf16[2,32,2560]{2,1,0:T(8,128)(2,1)S(1)}, u32[]{:S(2)}, u32[]{:S(2)}) collective-permute-start(bf16[2,32,2560]{2,1,0:T(8,128)(2,1)S(1)} %dynamic-slice_convert_fusion.7), channel_id=1, source_target_pairs={{0,32},{32,0},{1,33},{33,1},{2,34},{34,2},{3,35},{35,3},{4,36},{36... | collective-permute-start | bytes 983048 | tf_op jit(solution)/shard_map/ppermute | solution.py:22
  367.4 9.4 %collective-permute-start.42 = (bf16[2,16,2560]{2,1,0:T(8,128)(2,1)S(1)}, bf16[2,16,2560]{2,1,0:T(8,128)(2,1)S(1)}, u32[]{:S(2)}, u32[]{:S(2)}) collective-permute-start(bf16[2,16,2560]{2,1,0:T(8,128)(2,1)S(1)} %dynamic-slice_convert_fusion.14), channel_id=1, source_target_pairs={{0,16},{16,0},{1,17},{17,1},{2,18},{18,2},{3,19},{19,3},{4,20},{20... | collective-permute-start | bytes 491528 | tf_op jit(solution)/shard_map/ppermute | solution.py:22
  409.0 17.3 %collective-permute-start.50 = (bf16[2,2,16,2560]{3,2,1,0:T(8,128)(2,1)S(1)}, bf16[2,2,16,2560]{3,2,1,0:T(8,128)(2,1)S(1)}, u32[]{:S(2)}, u32[]{:S(2)}) collective-permute-start(bf16[2,2,16,2560]{3,2,1,0:T(8,128)(2,1)S(1)} %pad_maximum_fusion.15), channel_id=1, source_target_pairs={{0,16},{16,0},{1,17},{17,1},{2,18},{18,2},{3,19},{19,3},{4,20},{20... | collective-permute-start | bytes 983048 | tf_op jit(solution)/shard_map/ppermute | solution.py:22
  426.5 33.2 %collective-permute-start.51 = (bf16[2,2,32,2560]{3,2,1,0:T(8,128)(2,1)S(1)}, bf16[2,2,32,2560]{3,2,1,0:T(8,128)(2,1)S(1)}, u32[]{:S(2)}, u32[]{:S(2)}) collective-permute-start(bf16[2,2,32,2560]{3,2,1,0:T(8,128)(2,1)S(1)} %pad_maximum_fusion.8), channel_id=1, source_target_pairs={{0,32},{32,0},{1,33},{33,1},{2,34},{34,2},{3,35},{35,3},{4,36},{36... | collective-permute-start | bytes 1966088 | tf_op jit(solution)/shard_map/ppermute | solution.py:22
  463.1 12.8 %collective-permute-start.52 = (bf16[2,32,2560]{2,1,0:T(8,128)(2,1)S(1)}, bf16[2,32,2560]{2,1,0:T(8,128)(2,1)S(1)}, u32[]{:S(2)}, u32[]{:S(2)}) collective-permute-start(bf16[2,32,2560]{2,1,0:T(8,128)(2,1)S(1)} %dynamic-slice_convert_fusion.6), channel_id=1, source_target_pairs={{0,32},{32,0},{1,33},{33,1},{2,34},{34,2},{3,35},{35,3},{4,36},{36... | collective-permute-start | bytes 983048 | tf_op jit(solution)/shard_map/ppermute | solution.py:22
  476.0 10.3 %collective-permute-start.53 = (bf16[2,16,2560]{2,1,0:T(8,128)(2,1)S(1)}, bf16[2,16,2560]{2,1,0:T(8,128)(2,1)S(1)}, u32[]{:S(2)}, u32[]{:S(2)}) collective-permute-start(bf16[2,16,2560]{2,1,0:T(8,128)(2,1)S(1)} %dynamic-slice_convert_fusion.13), channel_id=1, source_target_pairs={{0,16},{16,0},{1,17},{17,1},{2,18},{18,2},{3,19},{19,3},{4,20},{20... | collective-permute-start | bytes 491528 | tf_op jit(solution)/shard_map/ppermute | solution.py:22
  517.7 16.4 %collective-permute-start.61 = (bf16[2,2,16,2560]{3,2,1,0:T(8,128)(2,1)S(1)}, bf16[2,2,16,2560]{3,2,1,0:T(8,128)(2,1)S(1)}, u32[]{:S(2)}, u32[]{:S(2)}) collective-permute-start(bf16[2,2,16,2560]{3,2,1,0:T(8,128)(2,1)S(1)} %pad_maximum_fusion.16), channel_id=1, source_target_pairs={{0,16},{16,0},{1,17},{17,1},{2,18},{18,2},{3,19},{19,3},{4,20},{20... | collective-permute-start | bytes 983048 | tf_op jit(solution)/shard_map/ppermute | solution.py:22
  534.3 34.4 %collective-permute-start.62 = (bf16[2,2,32,2560]{3,2,1,0:T(8,128)(2,1)S(1)}, bf16[2,2,32,2560]{3,2,1,0:T(8,128)(2,1)S(1)}, u32[]{:S(2)}, u32[]{:S(2)}) collective-permute-start(bf16[2,2,32,2560]{3,2,1,0:T(8,128)(2,1)S(1)} %pad_maximum_fusion.9), channel_id=1, source_target_pairs={{0,32},{32,0},{1,33},{33,1},{2,34},{34,2},{3,35},{35,3},{4,36},{36... | collective-permute-start | bytes 1966088 | tf_op jit(solution)/shard_map/ppermute | solution.py:22
  572.1 12.7 %collective-permute-start.63 = (bf16[2,32,2560]{2,1,0:T(8,128)(2,1)S(1)}, bf16[2,32,2560]{2,1,0:T(8,128)(2,1)S(1)}, u32[]{:S(2)}, u32[]{:S(2)}) collective-permute-start(bf16[2,32,2560]{2,1,0:T(8,128)(2,1)S(1)} %dynamic-slice_convert_fusion.5), channel_id=1, source_target_pairs={{0,32},{32,0},{1,33},{33,1},{2,34},{34,2},{3,35},{35,3},{4,36},{36... | collective-permute-start | bytes 983048 | tf_op jit(solution)/shard_map/ppermute | solution.py:22
  584.9 9.9 %collective-permute-start.64 = (bf16[2,16,2560]{2,1,0:T(8,128)(2,1)S(1)}, bf16[2,16,2560]{2,1,0:T(8,128)(2,1)S(1)}, u32[]{:S(2)}, u32[]{:S(2)}) collective-permute-start(bf16[2,16,2560]{2,1,0:T(8,128)(2,1)S(1)} %dynamic-slice_convert_fusion.12), channel_id=1, source_target_pairs={{0,16},{16,0},{1,17},{17,1},{2,18},{18,2},{3,19},{19,3},{4,20},{20... | collective-permute-start | bytes 491528 | tf_op jit(solution)/shard_map/ppermute | solution.py:22
  626.1 16.6 %collective-permute-start.72 = (bf16[2,2,16,2560]{3,2,1,0:T(8,128)(2,1)S(1)}, bf16[2,2,16,2560]{3,2,1,0:T(8,128)(2,1)S(1)}, u32[]{:S(2)}, u32[]{:S(2)}) collective-permute-start(bf16[2,2,16,2560]{3,2,1,0:T(8,128)(2,1)S(1)} %pad_maximum_fusion.17), channel_id=1, source_target_pairs={{0,16},{16,0},{1,17},{17,1},{2,18},{18,2},{3,19},{19,3},{4,20},{20... | collective-permute-start | bytes 983048 | tf_op jit(solution)/shard_map/ppermute | solution.py:22
  642.9 34.3 %collective-permute-start.73 = (bf16[2,2,32,2560]{3,2,1,0:T(8,128)(2,1)S(1)}, bf16[2,2,32,2560]{3,2,1,0:T(8,128)(2,1)S(1)}, u32[]{:S(2)}, u32[]{:S(2)}) collective-permute-start(bf16[2,2,32,2560]{3,2,1,0:T(8,128)(2,1)S(1)} %pad_maximum_fusion.10), channel_id=1, source_target_pairs={{0,32},{32,0},{1,33},{33,1},{2,34},{34,2},{3,35},{35,3},{4,36},{36... | collective-permute-start | bytes 1966088 | tf_op jit(solution)/shard_map/ppermute | solution.py:22
  680.7 12.2 %collective-permute-start.74 = (bf16[2,32,2560]{2,1,0:T(8,128)(2,1)S(1)}, bf16[2,32,2560]{2,1,0:T(8,128)(2,1)S(1)}, u32[]{:S(2)}, u32[]{:S(2)}) collective-permute-start(bf16[2,32,2560]{2,1,0:T(8,128)(2,1)S(1)} %dynamic-slice_convert_fusion.4), channel_id=1, source_target_pairs={{0,32},{32,0},{1,33},{33,1},{2,34},{34,2},{3,35},{35,3},{4,36},{36... | collective-permute-start | bytes 983048 | tf_op jit(solution)/shard_map/ppermute | solution.py:22
  694.5 10.8 %collective-permute-start.75 = (bf16[2,16,2560]{2,1,0:T(8,128)(2,1)}, bf16[2,16,2560]{2,1,0:T(8,128)(2,1)}, u32[]{:S(2)}, u32[]{:S(2)}) collective-permute-start(bf16[2,16,2560]{2,1,0:T(8,128)(2,1)} %dynamic-slice_convert_fusion.11), channel_id=1, source_target_pairs={{0,16},{16,0},{1,17},{17,1},{2,18},{18,2},{3,19},{19,3},{4,20},{20... | collective-permute-start | bytes 491528 | tf_op jit(solution)/shard_map/ppermute | solution.py:22
  717.1 35.5 %collective-permute-start.82 = (bf16[2560,320]{0,1:T(8,128)(2,1)}, bf16[2560,320]{0,1:T(8,128)(2,1)}, u32[]{:S(2)}, u32[]{:S(2)}) collective-permute-start(bf16[2560,320]{0,1:T(8,128)(2,1)} %dynamic-slice_convert_fusion), channel_id=1, source_target_pairs={{0,2},{2,0},{1,3},{3,1},{4,6},{6,4},{5,7},{7,5},{8,10},{10,8},{9,1... | collective-permute-start | bytes 4915208 | tf_op jit(solution)/shard_map/ppermute | solution.py:22
  724.0 63.7 %collective-permute-start.80 = (bf16[2560,320]{0,1:T(8,128)(2,1)}, bf16[2560,320]{0,1:T(8,128)(2,1)}, u32[]{:S(2)}, u32[]{:S(2)}) collective-permute-start(bf16[2560,320]{0,1:T(8,128)(2,1)} %dynamic-slice_convert_fusion.1), channel_id=1, source_target_pairs={{0,2},{2,0},{1,3},{3,1},{4,6},{6,4},{5,7},{7,5},{8,10},{10,8},{9,1... | collective-permute-start | bytes 4915208 | tf_op jit(solution)/shard_map/ppermute | solution.py:22
  755.6 38.2 %collective-permute-start.83 = (bf16[2560,160]{0,1:T(8,128)(2,1)S(1)}, bf16[2560,160]{0,1:T(8,128)(2,1)S(1)}, u32[]{:S(2)}, u32[]{:S(2)}) collective-permute-start(bf16[2560,160]{0,1:T(8,128)(2,1)S(1)} %dynamic-slice_convert_fusion.2), channel_id=1, source_target_pairs={{0,1},{1,0},{2,3},{3,2},{4,5},{5,4},{6,7},{7,6},{8,9},{9,8},{10,11... | collective-permute-start | bytes 2457608 | tf_op jit(solution)/shard_map/ppermute | solution.py:22
  (94 other events, 475.0 us)
where the time goes:
time: 806 us; the launch traced here: 796 us
  waiting for transfers between devices  556 us (69%)
  starting transfers between devices  153 us (19%)
  other arithmetic  30.5 us (4%)
  matrix products  23.8 us (3%)
  local copies, waits for them, and re-layouts  17.2 us (2%)
  blocking collectives  12.9 us (2%)
    ppermute x78, waiting for transfers between devices, swapped(): return lax.ppermute(block, axis, route)  543 us
    ppermute x78, starting transfers between devices, swapped(): return lax.ppermute(block, axis, route)  140 us
  transfers between devices with their start and end apart: 84, of which 78 were waited for; matrix products, arithmetic and copies ran while one was open for 2% of the time, Pallas kernels for 0%

commit v1 on v0

v1 whole, which is shorter than its diff:
```python
import jax
import jax.numpy as jnp
from jax import lax
from jax.experimental import pallas as pl
from jax.experimental.pallas import tpu as pltpu
from jax.sharding import PartitionSpec as P

D = 2560
FF_DEV = 640
GROUPS = 4
CAP = 2
MICRO = 4
CHUNKS = 4
ROWS = 16
HALF = D // 2
QUART = D // 4
SLOT_ROWS = CAP * ROWS
PIECE = FF_DEV // GROUPS
CHIPS = 32

gelu_coeff = 0.7978845608028654
gelu_cubic = 0.044715
epsilon = 1e-05

BF = jnp.bfloat16
F32 = jnp.float32
NT = (((1,), (1,)), ((), ()))

SLOT_MB, SLOT_LEN, MERGE, GROUP_OF, PLACE_OF, LENGTH = 0, 2, 4, 8, 12, 16


def choose(index, values):
    picked = values[0]
    for n in range(1, len(values)):
        picked = jnp.where(index == n, values[n], picked)
    return picked


def norm_scale(rows):
    return lax.rsqrt(jnp.mean(rows * rows, axis=-1, keepdims=True) + epsilon)


def kernel(
    table, tokens, cotangent, w_in_hbm, w_out_hbm, gain_ref,
    normed_out, masked_out, pre_out, act_out, grad_out,
    x_buf, u_buf, w_in, w_out, gains,
    pre_buf, pg_stage, act_stage, pg_all, act_all,
    merge_send_f, merge_own_f, merge_recv_f, rs_send_f, rs_recv_f, own_f,
    merge_send_b, merge_own_b, merge_recv_b, rs_send_b, rs_recv_b, own_b, final_recv,
    load_sem, x_sem, x_core_sem, u_sem, u_core_sem, core_send_sem,
    merge_sem_f, merge_sem_b, merge_send_sem, rs_sem, rs_send_sem, ag_send_sem,
    grads_sem, grads_send_sem, final_sem, final_send_sem, local_sem,
):
    t = lax.axis_index("section")
    r = lax.axis_index("replica")
    core = lax.rem(r, 2)
    chip = lax.div(r, 2)
    z = lax.div(r, 8)
    y = lax.rem(chip, 4)
    g = lax.rem(r, 4)
    part = lax.div(r, 4)
    last = lax.axis_size("section") - 1
    own_k = 2 * core + lax.rem(y + z, 2)
    own_i = lax.div(part, 4)
    own_j = lax.rem(part, 4)
    own_cols = pl.ds(pl.multiple_of(own_j * QUART, 128), QUART)
    mate = r + 1 - 2 * core
    my_half = pl.ds(pl.multiple_of(core * HALF, 128), HALF)
    mate_rows = pl.ds(pl.multiple_of((1 - core) * HALF, HALF), HALF)
    my_rows = pl.ds(pl.multiple_of(core * HALF, HALF), HALF)

    def to(section, replica):
        return dict(device_id=(section, replica), device_id_type=pl.DeviceIdType.MESH)

    in_load = pltpu.make_async_copy(w_in_hbm, w_in, load_sem.at[0])
    out_load = pltpu.make_async_copy(w_out_hbm, w_out, load_sem.at[1])
    x_load = pltpu.make_async_copy(tokens, x_buf, load_sem.at[2])
    u_load = pltpu.make_async_copy(cotangent, u_buf, load_sem.at[3])

    @pl.when(t == 0)
    def _():
        x_load.start()

    in_load.start()
    out_load.start()

    @pl.when(t == last)
    def _():
        u_load.start()

    gains[...] = gain_ref[...].astype(F32)
    in_load.wait()
    out_load.wait()

    @pl.when(t == 0)
    def _():
        x_load.wait()

    @pl.when(t == last)
    def _():
        u_load.wait()

    def gain_row(group):
        return choose(group, [gains[n : n + 1, :] for n in range(GROUPS)])

    def core_copy(buf, k, sem):
        view = buf.at[k, :, :, my_half]
        return pltpu.make_async_remote_copy(view, view, core_send_sem.at[0], sem.at[k], **to(t, mate))

    def arrive(buf, k, sem, core_sem):
        view = buf.at[k, :, :, my_half]
        pltpu.make_async_copy(view, view, sem.at[k]).wait()
        copy = core_copy(buf, k, core_sem)
        copy.start()
        copy.wait()

    def slot_rows(buf, k):
        rows = [buf[k, i] for i in range(MICRO)]
        return [choose(table[SLOT_MB + c], rows) for c in range(CAP)]

    def enter(k):
        gain = gain_row(g)
        parts = []
        for rows in slot_rows(x_buf, k):
            flat = rows.astype(F32)
            parts.append((flat * norm_scale(flat) * gain).astype(BF))
        normed = jnp.concatenate(parts, axis=0)
        pre = jnp.dot(normed, w_in[...], preferred_element_type=F32)
        pre_buf[k] = pre
        act = jax.nn.gelu(pre, approximate=True).astype(BF)
        for n in range(GROUPS):
            act_stage[n, k] = act[:, n * PIECE : (n + 1) * PIECE]
        return act

    def owner_of(k, i, jj):
        oz = 2 * i + core
        oy = 2 * jj + lax.rem(oz + k, 2)
        return oz * 8 + oy * 2 + lax.div(k, 2)

    def merge_copy(k, send, recv, sem):
        return pltpu.make_async_remote_copy(
            send.at[k], recv.at[k], merge_send_sem.at[0], sem.at[k], **to(t, mate)
        )

    def piece_copy(k, i, jj, send, recv, way):
        target = owner_of(k, i, jj)
        return target, pltpu.make_async_remote_copy(
            send.at[k, i, jj], recv.at[chip], rs_send_sem.at[way], rs_sem.at[way], **to(t, target)
        )

    def scatter(k, hidden, weight, extra, send, own, recv, rs_send, rs_recv, sem, way):
        width = HALF if extra is None else HALF + 128
        theirs = lax.dot_general(hidden, weight[mate_rows, :], NT, preferred_element_type=F32)
        send[k, :, 0:HALF] = theirs.astype(BF)
        if extra is not None:
            send[k, :, HALF:width] = extra
        copy = merge_copy(k, send, recv, sem)
        copy.start()
        mine = lax.dot_general(hidden, weight[my_rows, :], NT, preferred_element_type=F32)
        own[:, 0:HALF] = mine.astype(BF)
        if extra is not None:
            own[:, HALF:width] = extra
        copy.wait()
        for i in range(MICRO):
            which = table[MERGE + i]
            zero = jnp.zeros((ROWS, width), BF)
            merged = choose(
                which,
                [own[0:ROWS, :], own[ROWS:SLOT_ROWS, :], recv[k, 0:ROWS, :], recv[k, ROWS:SLOT_ROWS, :], zero],
            )
            for jj in range(2):
                rs_send[k, i, jj, :, 0:QUART] = merged[:, jj * QUART : (jj + 1) * QUART]
                if extra is not None:
                    rs_send[k, i, jj, :, QUART : QUART + 128] = merged[:, HALF:width]

        def send_piece(n, carry):
            i, jj = lax.div(n, 2), lax.rem(n, 2)
            target, remote = piece_copy(k, i, jj, rs_send, rs_recv, way)

            @pl.when(target != r)
            def _():
                remote.start()

            @pl.when(target == r)
            def _():
                pltpu.make_async_copy(rs_send.at[k, i, jj], rs_recv.at[chip], rs_sem.at[way]).start()

            return carry

        lax.fori_loop(0, 2 * MICRO, send_piece, 0)

    def scatter_done(rs_send, rs_recv, way):
        def wait_piece(n, carry):
            k, m = lax.div(n, 2 * MICRO), lax.rem(n, 2 * MICRO)
            target, remote = piece_copy(k, lax.div(m, 2), lax.rem(m, 2), rs_send, rs_recv, way)

            @pl.when(target != r)
            def _():
                remote.wait_send()

            return carry

        lax.fori_loop(0, CHUNKS * 2 * MICRO, wait_piece, 0)

    def total(recv):
        return jnp.sum(recv[...].astype(F32), axis=0)

    def live_rows(k, length):
        position = k * ROWS + lax.broadcasted_iota(jnp.int32, (ROWS, 1), 0)
        return position < length

    def spread_copy(n, source, buf, section, sem, way):
        a, b = lax.div(n, 4), lax.rem(n, 4)
        dz = 4 + (2 * lax.rem(a, 2) - 1) * lax.div(a + 1, 2)
        dy = 2 + (2 * lax.rem(b, 2) - 1) * lax.div(b + 1, 2)
        target = lax.rem(z + dz, 8) * 8 + lax.rem(y + dy, 4) * 2 + lax.div(own_j, 2)
        return pltpu.make_async_remote_copy(
            source, buf.at[own_k, own_i, :, own_cols], ag_send_sem.at[way], sem.at[own_k], **to(section, target)
        )

    def spread(source, buf, section, sem, way):
        def one(n, carry):
            spread_copy(n, source, buf, section, sem, way).start()
            return carry

        lax.fori_loop(0, CHIPS, one, 0)

    def spread_done(source, buf, section, sem, way):
        def one(n, carry):
            spread_copy(n, source, buf, section, sem, way).wait_send()
            return carry

        lax.fori_loop(0, CHIPS, one, 0)

    @pl.when(t < last)
    def _():
        def step(k, carry):
            @pl.when(t > 0)
            def _():
                arrive(x_buf, k, x_sem, x_core_sem)

            act = enter(k)
            scatter(
                k, act, w_out, None, merge_send_f, merge_own_f, merge_recv_f,
                rs_send_f, rs_recv_f, merge_sem_f, 0,
            )
            return carry

        lax.fori_loop(0, CHUNKS, step, 0)
        pltpu.make_async_copy(rs_recv_f, rs_recv_f, rs_sem.at[0]).wait()
        branch = total(rs_recv_f)
        live = live_rows(own_k, table[LENGTH + own_i]).astype(F32)
        held = x_buf[own_k, own_i, :, own_cols].astype(F32)
        own_f[...] = (held + live * branch).astype(BF)
        spread(own_f, x_buf, t + 1, x_sem, 0)

    def back(k, carry):
        @pl.when(t == last)
        def _():
            arrive(x_buf, k, x_sem, x_core_sem)
            enter(k)

        @pl.when(t < last)
        def _():
            arrive(u_buf, k, u_sem, u_core_sem)

        parts = []
        for c, rows in enumerate(slot_rows(u_buf, k)):
            live = live_rows(k, table[SLOT_LEN + c]).astype(F32)
            parts.append((rows.astype(F32) * live).astype(BF))
        masked = jnp.concatenate(parts, axis=0)
        act_grad = jnp.dot(masked, w_out[...], preferred_element_type=F32)
        pre = pre_buf[k]
        inner = gelu_coeff * (pre + gelu_cubic * pre * pre * pre)
        tangent = jnp.tanh(inner)
        slope = 0.5 * (1.0 + tangent) + 0.5 * pre * (1.0 - tangent * tangent) * gelu_coeff * (
            1.0 + 3.0 * gelu_cubic * pre * pre
        )
        pre_grad = (act_grad * slope).astype(BF)
        for n in range(GROUPS):
            pg_stage[n, k] = pre_grad[:, n * PIECE : (n + 1) * PIECE]
        dots = jnp.sum(pre_grad.astype(F32) * pre, axis=-1, keepdims=True)
        extra = jnp.broadcast_to(dots, (SLOT_ROWS, 128)).astype(BF)
        scatter(
            k, pre_grad, w_in, extra, merge_send_b, merge_own_b, merge_recv_b,
            rs_send_b, rs_recv_b, merge_sem_b, 1,
        )
        return carry

    lax.fori_loop(0, CHUNKS, back, 0)

    def grads_copy(d, stage, gathered, which):
        there = lax.rem(g + d, GROUPS)
        return pltpu.make_async_remote_copy(
            stage.at[there], gathered.at[g], grads_send_sem.at[which, d], grads_sem.at[which, d],
            **to(t, part * GROUPS + there),
        )

    for d in range(1, GROUPS):
        grads_copy(d, pg_stage, pg_all, 0).start()
        grads_copy(d, act_stage, act_all, 1).start()
    pg_all[g] = pg_stage[g]
    act_all[g] = act_stage[g]

    flat = x_buf[own_k, own_i].astype(F32)
    inv = norm_scale(flat)
    held = x_buf[own_k, own_i, :, own_cols].astype(F32)
    above = u_buf[own_k, own_i, :, own_cols].astype(F32)
    gain_own = choose(
        table[GROUP_OF + own_i], [gains[n : n + 1, own_cols] for n in range(GROUPS)]
    )
    pltpu.make_async_copy(rs_recv_b, rs_recv_b, rs_sem.at[1]).wait()
    summed = total(rs_recv_b)
    pulled = summed[:, 0:QUART] * gain_own
    row_dot = summed[:, QUART : QUART + 1] * (1.0 / D)
    own_b[...] = (above + inv * pulled - held * (inv * inv * row_dot)).astype(BF)

    def final_copy(n):
        target = own_k * ROWS + n
        return target, pltpu.make_async_remote_copy(
            own_b, final_recv.at[own_j], final_send_sem.at[0], final_sem.at[0], **to(own_i, target)
        )

    @pl.when(t > 0)
    def _():
        spread(own_b, u_buf, t - 1, u_sem, 1)

    @pl.when(t == 0)
    def _():
        def one(n, carry):
            target, copy = final_copy(n)
            here = (target == r) & (own_i == 0)

            @pl.when(jnp.logical_not(here))
            def _():
                copy.start()

            @pl.when(here)
            def _():
                pltpu.make_async_copy(own_b, final_recv.at[own_j], final_sem.at[0]).start()

            return carry

        lax.fori_loop(0, ROWS, one, 0)

    def gather_rows(k, carry):
        for i in range(MICRO):
            rows = x_buf[k, i].astype(F32)
            gain = gain_row(table[GROUP_OF + i])
            normed_out[k, i] = (rows * norm_scale(rows) * gain).astype(BF)
            live = live_rows(k, table[LENGTH + i]).astype(F32)
            masked_out[k, i] = (u_buf[k, i].astype(F32) * live).astype(BF)
        return carry

    lax.fori_loop(0, CHUNKS, gather_rows, 0)

    for d in range(1, GROUPS):
        grads_copy(d, pg_stage, pg_all, 0).wait()
        grads_copy(d, act_stage, act_all, 1).wait()

    def gather_hidden(k, carry):
        for gathered, out in ((pg_all, pre_out), (act_all, act_out)):
            pieces = [
                gathered[n, k, c * ROWS : (c + 1) * ROWS, :] for n in range(GROUPS) for c in range(CAP)
            ]
            for i in range(MICRO):
                out[k, i] = choose(table[PLACE_OF + i], pieces)
        return carry

    lax.fori_loop(0, CHUNKS, gather_hidden, 0)

    @pl.when(t < last)
    def _():
        scatter_done(rs_send_f, rs_recv_f, 0)
        spread_done(own_f, x_buf, t + 1, x_sem, 0)

    scatter_done(rs_send_b, rs_recv_b, 1)

    @pl.when(t > 0)
    def _():
        spread_done(own_b, u_buf, t - 1, u_sem, 1)

    pltpu.make_async_copy(final_recv, final_recv, final_sem.at[0]).wait()
    mine = lax.broadcasted_iota(jnp.int32, (ROWS, 1), 0) == lax.rem(r, ROWS)
    for j in range(4):
        rows = jnp.where(mine, final_recv[j].astype(F32), 0.0)
        grad_out[:, j * QUART : (j + 1) * QUART] = jnp.sum(rows, axis=0, keepdims=True).astype(BF)

    @pl.when(t == 0)
    def _():
        def one(n, carry):
            target, copy = final_copy(n)

            @pl.when(jnp.logical_not((target == r) & (own_i == 0)))
            def _():
                copy.wait_send()

            return carry

        lax.fori_loop(0, ROWS, one, 0)


def small_table(wiring, lengths):
    t = lax.axis_index("section")
    g = lax.axis_index("replica") % GROUPS
    routes = lax.dynamic_index_in_dim(wiring[:, :, 0], t, 0, keepdims=False)
    order = jnp.arange(MICRO, dtype=jnp.int32)
    earlier = (routes[:, None] == routes[None, :]) & (order[None, :] < order[:, None])
    slot = jnp.sum(earlier.astype(jnp.int32), axis=1)
    here = (routes[None, :] == g) & (slot[None, :] == jnp.arange(CAP)[:, None])
    slot_mb = jnp.sum(jnp.where(here, order[None, :], 0), axis=1)
    slot_len = jnp.sum(jnp.where(here, lengths[None, :], 0), axis=1)
    merge = jnp.where(routes == g, slot, jnp.where(routes == (g ^ 1), CAP + slot, 2 * CAP))
    return jnp.concatenate([slot_mb, slot_len, merge, routes, routes * CAP + slot, lengths]).astype(jnp.int32)


def body(tokens, cotangent, wiring, lengths, in_proj, out_proj, section_gain):
    table = small_table(wiring, lengths)
    both = lax.all_gather(jnp.stack([tokens, cotangent]), "replica", axis=2, tiled=True)
    both = both.reshape(2, MICRO, CHUNKS, ROWS, D).transpose(0, 2, 1, 3, 4)
    vmem = pl.BlockSpec(memory_space=pltpu.VMEM)
    hbm = pl.BlockSpec(memory_space=pl.ANY)
    dma = pltpu.SemaphoreType.DMA
    normed, masked, pre_grad, act, grad = pl.pallas_call(
        kernel,
        name="relay",
        out_shape=(
            jax.ShapeDtypeStruct((CHUNKS, MICRO, ROWS, D), BF),
            jax.ShapeDtypeStruct((CHUNKS, MICRO, ROWS, D), BF),
            jax.ShapeDtypeStruct((CHUNKS, MICRO, ROWS, PIECE), BF),
            jax.ShapeDtypeStruct((CHUNKS, MICRO, ROWS, PIECE), BF),
            jax.ShapeDtypeStruct((1, D), BF),
        ),
        in_specs=[pl.BlockSpec(memory_space=pltpu.SMEM), hbm, hbm, hbm, hbm, vmem],
        out_specs=(vmem,) * 5,
        scratch_shapes=[
            pltpu.VMEM((CHUNKS, MICRO, ROWS, D), BF),
            pltpu.VMEM((CHUNKS, MICRO, ROWS, D), BF),
            pltpu.VMEM((D, FF_DEV), BF),
            pltpu.VMEM((D, FF_DEV), BF),
            pltpu.VMEM((GROUPS, D), F32),
            pltpu.VMEM((CHUNKS, SLOT_ROWS, FF_DEV), F32),
            pltpu.VMEM((GROUPS, CHUNKS, SLOT_ROWS, PIECE), BF),
            pltpu.VMEM((GROUPS, CHUNKS, SLOT_ROWS, PIECE), BF),
            pltpu.VMEM((GROUPS, CHUNKS, SLOT_ROWS, PIECE), BF),
            pltpu.VMEM((GROUPS, CHUNKS, SLOT_ROWS, PIECE), BF),
            pltpu.VMEM((CHUNKS, SLOT_ROWS, HALF), BF),
            pltpu.VMEM((SLOT_ROWS, HALF), BF),
            pltpu.VMEM((CHUNKS, SLOT_ROWS, HALF), BF),
            pltpu.VMEM((CHUNKS, MICRO, 2, ROWS, QUART), BF),
            pltpu.VMEM((CHIPS, ROWS, QUART), BF),
            pltpu.VMEM((ROWS, QUART), BF),
            pltpu.VMEM((CHUNKS, SLOT_ROWS, HALF + 128), BF),
            pltpu.VMEM((SLOT_ROWS, HALF + 128), BF),
            pltpu.VMEM((CHUNKS, SLOT_ROWS, HALF + 128), BF),
            pltpu.VMEM((CHUNKS, MICRO, 2, ROWS, QUART + 128), BF),
            pltpu.VMEM((CHIPS, ROWS, QUART + 128), BF),
            pltpu.VMEM((ROWS, QUART), BF),
            pltpu.VMEM((4, ROWS, QUART), BF),
            dma((4,)),
            dma((CHUNKS,)),
            dma((CHUNKS,)),
            dma((CHUNKS,)),
            dma((CHUNKS,)),
            dma((1,)),
            dma((CHUNKS,)),
            dma((CHUNKS,)),
            dma((1,)),
            dma((2,)),
            dma((2,)),
            dma((2,)),
            dma((2, GROUPS)),
            dma((2, GROUPS)),
            dma((1,)),
            dma((1,)),
            dma((1,)),
        ],
        compiler_params=pltpu.CompilerParams(
            has_side_effects=True, vmem_limit_bytes=48 * 1024 * 1024
        ),
    )(table, both[0], both[1], in_proj[0, 0], out_proj[0, 0], section_gain[0])
    rows = CHUNKS * MICRO * ROWS
    contract = (((0,), (0,)), ((), ()))
    in_grad = lax.dot_general(
        normed.reshape(rows, D), pre_grad.reshape(rows, PIECE), contract, preferred_element_type=F32
    )
    out_grad = lax.dot_general(
        masked.reshape(rows, D), act.reshape(rows, PIECE), contract, preferred_element_type=F32
    )
    return grad[None], in_grad.astype(BF)[None], out_grad.astype(BF)[None]


def solution(mesh):
    in_specs = (
        P(None, "replica", None),
        P(None, "replica", None),
        P(),
        P(),
        P("section", "replica", None, None),
        P("section", "replica", None, None),
        P("section", None, None),
    )
    out_specs = (
        P("section", "replica", None),
        P("section", None, "replica"),
        P("section", None, "replica"),
    )
    return jax.shard_map(body, mesh=mesh, in_specs=in_specs, out_specs=out_specs, check_vma=False)
```

time: 806 us -> 379 us (0.47)
  the two profiles are of different devices: /device:TPU:1 before, /device:TPU:229 now
where the time goes in v1:
time: 379 us
  Pallas kernels  278 us (73%)
  waiting for transfers between devices  77.4 us (20%)
  between operations  14.1 us (4%)
  local copies, waits for them, and re-layouts  4.34 us (1%)
    pallas_call x1, Pallas kernels, body(): pl.pallas_call(kernel, name='relay', out_shape=(jax.ShapeDtypeStruct((CHU...  278 us
    all_gather x1, waiting for transfers between devices, body(): lax.all_gather(jnp.stack([tokens, cotangent]), 'replica', axis=2, tiled=T...  77.4 us
  transfers between devices with their start and end apart: 1, of which 1 were waited for; matrix products, arithmetic and copies ran while one was open for 1% of the time, Pallas kernels for 0%

profile of v1, /device:TPU:229, one launch (start us, length us, event | category | flops | bytes accessed | tf_op | source)
XLA Modules:
  0.0 379.0 jit_solution(14324965546334057844)
XLA Ops:
  7.2 0.0 all-gather.2.cloned.1.call-start
  7.2 1.4 pad_maximum_fusion
  8.6 0.0 all-gather.2.cloned.1.call-update
  8.6 0.7 broadcast_compare_fusion
  9.3 0.2 convert_reduce_fusion
  9.5 0.8 select_reduce_fusion
  10.3 0.7 concatenate.3.table
  11.0 77.4 %all-gather.2.cloned.1.call-done = bf16[2,4,64,2560]{3,1,2,0:T(4,128)(2,1)} async-done(((bf16[2,4,1,2560]{3,1,2,0:T(4,128)(2,1)}), bf16[2,4,64,2560]{3,1,2,0:T(4,128)(2,1)}) %all-gather.2.cloned.1.call-update) | async-done | bytes 2621456 | tf_op jit(solution)/shard_map/all_gather | solution.py:419
  88.4 2.3 copy.20
  90.7 0.0 copy-start
  90.7 0.2 slice_bitcast_fusion
  90.9 0.5 copy-done
  91.4 277.5 %relay.1 = (bf16[4,4,16,2560]{3,2,1,0:T(8,128)(2,1)S(1)}, bf16[4,4,16,2560]{3,2,1,0:T(8,128)(2,1)S(1)}, bf16[4,4,16,160]{3,2,1,0:T(8,128)(2,1)S(1)}, bf16[4,4,16...) custom-call(s32[20]{0:T(128)S(1)} %concatenate.3.table, bf16[4,4,16,2560]{3,2,1,0:T(8,128)(2,1)S(1)} %get-tuple-element.18.tokens, ...), custom_call_target="tpu_custom_call" | custom-call | tf_op jit(solution)/shard_map/relay/pallas_call | solution.py:424
  369.0 1.3 fusion.3
  370.3 1.3 fusion.2
  371.6 0.6 copy.22
  (1 shorter events, 0.0 us)
Async XLA Ops:
  7.2 81.2 %all-gather.2.cloned.1.call-start = ((), (), s32[]{:S(2)}) async-start(), calls=%async_computation | async-start | bytes 2662400 | tf_op jit(solution)/shard_map/all_gather | solution.py:419
  90.7 0.7 copy-start
Sparse Core Ops, SparseCore 0:
  11.3 77.0 all-gather.1

commit v2 on v1

v2 whole, which is shorter than its diff:
```python
import jax
import jax.numpy as jnp
from jax import lax
from jax.experimental import pallas as pl
from jax.experimental.pallas import tpu as pltpu
from jax.sharding import PartitionSpec as P

D = 2560
FF_DEV = 640
GROUPS = 4
CAP = 2
MICRO = 4
CHUNKS = 4
ROWS = 16
HALF = D // 2
QUART = D // 4
SLOT_ROWS = CAP * ROWS
PIECE = FF_DEV // GROUPS
CHIPS = 32
LINE = 8

gelu_coeff = 0.7978845608028654
gelu_cubic = 0.044715
epsilon = 1e-05

BF = jnp.bfloat16
F32 = jnp.float32
NT = (((1,), (1,)), ((), ()))

def choose(index, values):
    picked = values[0]
    for n in range(1, len(values)):
        picked = jnp.where(index == n, values[n], picked)
    return picked


def norm_scale(rows):
    return lax.rsqrt(jnp.mean(rows * rows, axis=-1, keepdims=True) + epsilon)


def kernel(
    wiring, lengths, tokens, cotangent, w_in_hbm, w_out_hbm, gain_hbm,
    normed_out, masked_out, pre_out, act_out, grad_out,
    x_buf, u_buf, w_in, w_out, gain_rows, gains, entry_rows, entry_send, entry_recv,
    h_buf, pre_buf, inv_buf, act_buf, back_buf, pg_stage, act_stage, pg_all, act_all,
    merge_send_f, merge_own, merge_recv_f, line_send_f, line_recv_f, rs_send_f, rs_recv_f, own_f, held_recv,
    merge_send_b, merge_recv_b, line_send_b, line_recv_b, rs_send_b, rs_recv_b, own_b, above_recv, final_own, final_recv,
    load_sem, go_sem, entry_sem, entry_send_sem, x_sem, x_core_sem, u_sem, u_core_sem, core_send_sem,
    merge_sem_f, merge_sem_b, merge_send_sem, line_sem, line_send_sem, rs_sem, rs_send_sem, ag_send_sem,
    pass_sem, pass_send_sem, grads_sem, grads_send_sem, final_sem, final_send_sem,
):
    t = lax.axis_index("section")
    r = lax.axis_index("replica")
    core = lax.rem(r, 2)
    other = 1 - core
    chip = lax.div(r, 2)
    z = lax.div(r, 8)
    y = lax.rem(chip, 4)
    g = lax.rem(r, 4)
    part = lax.div(r, 4)
    last = lax.axis_size("section") - 1
    own_k = lax.rem(z + 2 * core, 4)
    own_i = 2 * lax.div(z, 4) + lax.rem(y, 2)
    own_j = 2 * core + lax.div(y, 2)
    own_cols = pl.ds(pl.multiple_of(own_j * QUART, 128), QUART)
    own_turn = jnp.maximum(own_k - 2, 0)
    mate = r + 1 - 2 * core
    my_half = pl.ds(pl.multiple_of(core * HALF, 128), HALF)
    mate_half = pl.ds(pl.multiple_of(other * HALF, 128), HALF)
    mate_rows = pl.ds(pl.multiple_of(other * HALF, HALF), HALF)
    my_rows = pl.ds(pl.multiple_of(core * HALF, HALF), HALF)

    routes = [wiring[t, 0, i] for i in range(MICRO)]
    lens = [lengths[i] for i in range(MICRO)]
    slots = []
    for i in range(MICRO):
        taken = jnp.int32(0)
        for e in range(i):
            taken = taken + jnp.where(routes[e] == routes[i], 1, 0)
        slots.append(taken)
    slot_mb, slot_len = [], []
    for c in range(CAP):
        number, length = jnp.int32(0), jnp.int32(0)
        for i in range(MICRO):
            here = (routes[i] == g) & (slots[i] == c)
            number = jnp.where(here, i, number)
            length = jnp.where(here, lens[i], length)
        slot_mb.append(number)
        slot_len.append(length)
    mate_g = g + 1 - 2 * core
    merge_from = [
        jnp.where(routes[i] == g, slots[i], jnp.where(routes[i] == mate_g, CAP + slots[i], 2 * CAP))
        for i in range(MICRO)
    ]

    def to(section, replica):
        return dict(device_id=(section, replica), device_id_type=pl.DeviceIdType.MESH)

    def start_or_keep(target_section, target, remote, source, dest, sem):
        here = (target == r) & (target_section == t)

        @pl.when(jnp.logical_not(here))
        def _():
            remote.start()

        @pl.when(here)
        def _():
            pltpu.make_async_copy(source, dest, sem).start()

    def wait_sent(target_section, target, remote):
        @pl.when(jnp.logical_not((target == r) & (target_section == t)))
        def _():
            remote.wait_send()

    def owner_z(k, oc):
        return lax.rem(k + 2 * oc, 4)

    entry_z = [owner_z(lax.div(r, ROWS), oc) for oc in range(2)]

    def entry_copy(n):
        i, j = n // 4, n % 4
        oy = 2 * (j % 2) + i % 2
        target = (entry_z[j // 2] + 4 * (i // 2)) * 8 + oy * 2 + j // 2
        source, dest = entry_send.at[i, j], entry_recv.at[lax.rem(r, ROWS)]
        return target, source, dest, pltpu.make_async_remote_copy(
            source, dest, entry_send_sem.at[0], entry_sem.at[0], **to(t, target)
        )

    in_load = pltpu.make_async_copy(w_in_hbm, w_in, load_sem.at[0])
    out_load = pltpu.make_async_copy(w_out_hbm, w_out, load_sem.at[1])
    gain_load = pltpu.make_async_copy(gain_hbm, gain_rows, load_sem.at[2])
    ends = (t == 0) | (t == last)

    @pl.when(t == 0)
    def _():
        pltpu.make_async_copy(tokens, entry_rows, load_sem.at[3]).start()

    @pl.when(t == last)
    def _():
        pltpu.make_async_copy(cotangent, entry_rows, load_sem.at[3]).start()

    gain_load.start()
    in_load.start()
    out_load.start()

    barrier = pltpu.get_barrier_semaphore()
    planes = lax.axis_size("section")
    replicas = lax.axis_size("replica")

    def tell_line(n, carry):
        for shift in (1, planes - 1):
            there = lax.rem(t + shift, planes)
            pl.semaphore_signal(barrier, inc=1, **to(there, n * 8 + y * 2 + other))
        return carry

    def tell_plane(n, carry):
        pl.semaphore_signal(barrier, inc=1, **to(t, lax.rem(r + n, replicas)))
        return carry

    lax.fori_loop(1, replicas, tell_plane, 0)
    lax.fori_loop(0, LINE, tell_line, 0)
    for shift in (1, planes - 1):
        pl.semaphore_signal(barrier, inc=1, **to(lax.rem(t + shift, planes), r))

    @pl.when(t > 0)
    def _():
        final_z = [owner_z(lax.div(r, ROWS), oc) for oc in range(2)]
        for j in range(4):
            oy = 2 * (j % 2) + lax.rem(t, 2)
            target = (final_z[j // 2] + 4 * lax.div(t, 2)) * 8 + oy * 2 + j // 2
            pl.semaphore_signal(barrier, inc=1, **to(0, target))

    @pl.when(ends)
    def _():
        pltpu.make_async_copy(tokens, entry_rows, load_sem.at[3]).wait()
        for i in range(MICRO):
            row = entry_rows[i : i + 1, :].astype(F32)
            for j in range(4):
                entry_send[i, j] = row[:, j * QUART : (j + 1) * QUART]

    gain_load.wait()
    gains[...] = gain_rows[...].astype(F32)
    pl.semaphore_wait(barrier, replicas - 1 + 2 * LINE + 2 + jnp.where((t == 0) & (own_i > 0), ROWS, 0))

    @pl.when(ends)
    def _():
        for n in range(MICRO * 4):
            target, source, dest, copy = entry_copy(n)
            start_or_keep(t, target, copy, source, dest, entry_sem.at[0])

    def entered():
        pltpu.make_async_copy(entry_recv, entry_recv, entry_sem.at[0]).wait()
        return entry_recv[...].reshape(ROWS, QUART).astype(BF)

    def gain_row(group):
        return choose(group, [gains[n : n + 1, :] for n in range(GROUPS)])

    def arrive(buf, k, sem, core_sem):
        view = buf.at[k, :, :, mate_half]
        pltpu.make_async_copy(view, view, sem.at[k]).wait()
        copy = pltpu.make_async_remote_copy(view, view, core_send_sem.at[0], core_sem.at[k], **to(t, mate))
        copy.start()
        return copy

    def slot_rows(buf, k, cols):
        rows = [buf[k, i, :, cols] for i in range(MICRO)]
        return jnp.concatenate([choose(slot_mb[c], rows) for c in range(CAP)], axis=0)

    def gain_part(cols):
        return choose(g, [gains[n : n + 1, cols] for n in range(GROUPS)])

    def slot_live(k):
        return jnp.concatenate([live_rows(k, slot_len[c]).astype(F32) for c in range(CAP)], axis=0)

    def x_stage(k):
        copy = arrive(x_buf, k, x_sem, x_core_sem)

        def half(cols, rows):
            held = slot_rows(x_buf, k, cols)
            h_buf[k, :, cols] = held
            flat = held.astype(F32)
            scaled = (flat * gain_part(cols)).astype(BF)
            squares = jnp.sum(flat * flat, axis=-1, keepdims=True)
            return squares, jnp.dot(scaled, w_in[rows, :], preferred_element_type=F32)

        mine = half(mate_half, mate_rows)
        copy.wait()
        theirs = half(my_half, my_rows)
        inv = lax.rsqrt((mine[0] + theirs[0]) * (1.0 / D) + epsilon)
        inv_buf[k] = jnp.broadcast_to(inv, (SLOT_ROWS, 128))
        pre = (mine[1] + theirs[1]) * inv
        pre_buf[k] = pre
        act = jax.nn.gelu(pre, approximate=True).astype(BF)
        act_buf[k] = act
        return act

    def u_stage(k):
        copy = arrive(u_buf, k, u_sem, u_core_sem)
        live = slot_live(k)

        def half(cols, rows):
            masked = (slot_rows(u_buf, k, cols).astype(F32) * live).astype(BF)
            return jnp.dot(masked, w_out[rows, :], preferred_element_type=F32)

        mine = half(mate_half, mate_rows)
        copy.wait()
        back_buf[k] = mine + half(my_half, my_rows)

    def merge_copy(k, send, recv, sem):
        return pltpu.make_async_remote_copy(
            send.at[k], recv.at[k], merge_send_sem.at[0], sem.at[k], **to(t, mate)
        )

    line_base = z * 8 + other

    def scatter(k, half, send, recv, line_send, line_recv, sem, way):
        send[k] = half(mate_rows, mate_half)
        copy = merge_copy(k, send, recv, sem)
        copy.start()
        merge_own[...] = half(my_rows, my_half)
        copy.wait()
        for i in range(MICRO):
            merged = choose(
                merge_from[i],
                [
                    merge_own[0:ROWS, :], merge_own[ROWS:SLOT_ROWS, :],
                    recv[k, 0:ROWS, :], recv[k, ROWS:SLOT_ROWS, :], jnp.zeros((ROWS, HALF), BF),
                ],
            )
            for jj in range(2):
                line_send[k, 2 * jj + i % 2, i // 2] = merged[:, jj * QUART : (jj + 1) * QUART]
        for there in range(4):
            pltpu.make_async_remote_copy(
                line_send.at[k, there], line_recv.at[k, y], line_send_sem.at[way], line_sem.at[way, k],
                **to(t, line_base + 2 * there),
            ).start()

    def relay(k, section, line_recv, rs_send, rs_recv, way, slot):
        pltpu.make_async_copy(line_recv.at[k], line_recv.at[k], line_sem.at[way, k]).wait()
        base = owner_z(k, other) * 8 + y * 2 + other
        for n in range(2):
            pieces = [line_recv[k, e, n].astype(F32) for e in range(4)]
            rs_send[k, n] = ((pieces[0] + pieces[1]) + (pieces[2] + pieces[3])).astype(BF)
            pltpu.make_async_remote_copy(
                rs_send.at[k, n], rs_recv.at[z], rs_send_sem.at[way], rs_sem.at[slot],
                **to(section, base + 32 * n),
            ).start()

    def relay_turn(k, section, line_recv, rs_send, rs_recv, way, slot):
        @pl.when(k > 0)
        def _():
            relay(k - 1, section, line_recv, rs_send, rs_recv, way, slot)

        @pl.when(k == CHUNKS - 1)
        def _():
            relay(k, section, line_recv, rs_send, rs_recv, way, slot)

    def scatter_done(line_send, rs_send, way):
        pltpu.make_async_copy(line_send, line_send, line_send_sem.at[way]).wait()
        pltpu.make_async_copy(rs_send, rs_send, rs_send_sem.at[way]).wait()

    def live_rows(k, length):
        position = k * ROWS + lax.broadcasted_iota(jnp.int32, (ROWS, 1), 0)
        return position < length

    spread_z = [lax.rem(z + dz, 8) * 8 + other for dz in (4, 3, 5, 2, 6, 1, 7, 0)]
    spread_y = [lax.rem(y + dy, 4) * 2 for dy in (2, 1, 3, 0)]

    def spread(source, buf, sem, way):
        for base in spread_z:
            for add in spread_y:
                pltpu.make_async_remote_copy(
                    source, buf.at[own_k, own_i, :, own_cols], ag_send_sem.at[way], sem.at[own_k],
                    **to(t, base + add),
                ).start()

    def spread_done(source, way):
        def one(n, carry):
            pltpu.make_async_copy(source, source, ag_send_sem.at[way]).wait()
            return carry

        lax.fori_loop(0, CHIPS, one, 0)

    def pass_copy(source, dest, section, way):
        return pltpu.make_async_remote_copy(
            source, dest, pass_send_sem.at[way], pass_sem.at[way], **to(section, r)
        )

    def pass_on():
        return pass_copy(own_f, held_recv, t + 1, 0)

    def pass_above():
        return pass_copy(own_b, above_recv, t - 1, 1)

    def received(dest, way):
        pltpu.make_async_copy(dest, dest, pass_sem.at[way]).wait()

    def combined(before, pieces, slot):
        pltpu.make_async_copy(pieces, pieces, rs_sem.at[slot]).wait()
        return (before.astype(F32) + jnp.sum(pieces[...].astype(F32), axis=0)).astype(BF)

    def own_forward():
        @pl.when(t == 0)
        def _():
            own_f[...] = entered()

            @pl.when(own_k > 0)
            def _():
                pl.semaphore_wait(go_sem, 1)

        @pl.when(t > 0)
        def _():
            received(held_recv, 0)
            own_f[...] = combined(held_recv[...], rs_recv_f, 0)

        spread(own_f, x_buf, x_sem, 0)

        @pl.when((t == 0) & (own_k < CHUNKS - 1))
        def _():
            pl.semaphore_signal(go_sem, inc=1, **to(t, lax.rem(r + 8, replicas)))

        @pl.when(t < last)
        def _():
            pass_on().start()


    def own_backward():
        @pl.when(t == last)
        def _():
            own_b[...] = entered()

        @pl.when(t < last)
        def _():
            received(above_recv, 1)
            own_b[...] = combined(above_recv[...], rs_recv_b.at[0], 1)

        spread(own_b, u_buf, u_sem, 1)

        @pl.when(t > 0)
        def _():
            pass_above().start()

    def gather_normed(k, carry):
        for i in range(MICRO):
            rows = x_buf[k, i].astype(F32)
            gain = gain_row(routes[i])
            normed_out[k, i] = (rows * norm_scale(rows) * gain).astype(BF)
        return carry

    def gather_masked(k, carry):
        for i in range(MICRO):
            live = live_rows(k, lens[i]).astype(F32)
            masked_out[k, i] = (u_buf[k, i].astype(F32) * live).astype(BF)
        return carry

    def grads_copy(d, stage, gathered, which):
        there = lax.rem(g + d, GROUPS)
        return pltpu.make_async_remote_copy(
            stage.at[there], gathered.at[g], grads_send_sem.at[which, d], grads_sem.at[which, d],
            **to(t, part * GROUPS + there),
        )

    def send_act():
        for d in range(1, GROUPS):
            grads_copy(d, act_stage, act_all, 1).start()

    def split_act(k, carry):
        for n in range(GROUPS):
            act_stage[n, k] = act_buf[k, :, n * PIECE : (n + 1) * PIECE]
        return carry

    @pl.when(t == last)
    def _():
        own_backward()
        out_load.wait()

        def step(k, carry):
            u_stage(k)
            return carry

        lax.fori_loop(0, CHUNKS, step, 0)
        lax.fori_loop(0, CHUNKS, gather_masked, 0)
        in_load.wait()

    @pl.when(t < last)
    def _():
        in_load.wait()
        out_load.wait()

        def step(k, carry):
            @pl.when(k == own_turn)
            def _():
                own_forward()

            act = (x_stage(k).astype(F32) * slot_live(k)).astype(BF)

            def half(rows, cols):
                return lax.dot_general(act, w_out[rows, :], NT, preferred_element_type=F32).astype(BF)

            scatter(k, half, merge_send_f, merge_recv_f, line_send_f, line_recv_f, merge_sem_f, 0)
            relay_turn(k, t + 1, line_recv_f, rs_send_f, rs_recv_f, 0, 0)
            return carry

        lax.fori_loop(0, CHUNKS, step, 0)
        lax.fori_loop(0, CHUNKS, split_act, 0)
        send_act()
        lax.fori_loop(0, CHUNKS, gather_normed, 0)

    back_section = jnp.maximum(t - 1, 0)
    back_slot = jnp.where(t == 0, 1, 0)

    def back(k, carry):
        @pl.when((t == last) & (k == own_turn))
        def _():
            own_forward()

        @pl.when((t < last) & (k == own_turn))
        def _():
            own_backward()

        @pl.when(t == last)
        def _():
            x_stage(k)

        @pl.when(t < last)
        def _():
            u_stage(k)

        pre = pre_buf[k]
        inner = gelu_coeff * (pre + gelu_cubic * pre * pre * pre)
        tangent = jnp.tanh(inner)
        slope = 0.5 * (1.0 + tangent) + 0.5 * pre * (1.0 - tangent * tangent) * gelu_coeff * (
            1.0 + 3.0 * gelu_cubic * pre * pre
        )
        pre_grad = (back_buf[k] * slope).astype(BF)
        inv = inv_buf[k, :, 0:1]
        dots = jnp.sum(pre_grad.astype(F32) * pre, axis=-1, keepdims=True) * (inv * inv * (1.0 / D))

        def half(rows, cols):
            value = lax.dot_general(pre_grad, w_in[rows, :], NT, preferred_element_type=F32)
            return (value * inv * gain_part(cols) - h_buf[k, :, cols].astype(F32) * dots).astype(BF)

        scatter(k, half, merge_send_b, merge_recv_b, line_send_b, line_recv_b, merge_sem_b, 1)
        for n in range(GROUPS):
            pg_stage[n, k] = pre_grad[:, n * PIECE : (n + 1) * PIECE]
        relay_turn(k, back_section, line_recv_b, rs_send_b, rs_recv_b.at[back_slot], 1, 1 + back_slot)
        return carry

    lax.fori_loop(0, CHUNKS, back, 0)

    for d in range(1, GROUPS):
        grads_copy(d, pg_stage, pg_all, 0).start()

    @pl.when(t == last)
    def _():
        lax.fori_loop(0, CHUNKS, split_act, 0)
        send_act()
        lax.fori_loop(0, CHUNKS, gather_normed, 0)

    @pl.when(t < last)
    def _():
        lax.fori_loop(0, CHUNKS, gather_masked, 0)

    pg_all[g] = pg_stage[g]
    act_all[g] = act_stage[g]

    def final_copy(n):
        target = own_k * ROWS + n
        return target, pltpu.make_async_remote_copy(
            final_own, final_recv.at[own_j], final_send_sem.at[0], final_sem.at[0], **to(own_i, target)
        )

    @pl.when(t == 0)
    def _():
        final_own[...] = combined(own_b[...], rs_recv_b.at[1], 2)

        def one(n, carry):
            target, copy = final_copy(n)
            start_or_keep(own_i, target, copy, final_own, final_recv.at[own_j], final_sem.at[0])
            return carry

        lax.fori_loop(0, ROWS, one, 0)

    for d in range(1, GROUPS):
        grads_copy(d, pg_stage, pg_all, 0).wait()
        grads_copy(d, act_stage, act_all, 1).wait()

    def gather_hidden(k, carry):
        for gathered, out in ((pg_all, pre_out), (act_all, act_out)):
            pieces = [
                gathered[n, k, c * ROWS : (c + 1) * ROWS, :] for n in range(GROUPS) for c in range(CAP)
            ]
            for i in range(MICRO):
                out[k, i] = choose(routes[i] * CAP + slots[i], pieces)
        return carry

    lax.fori_loop(0, CHUNKS, gather_hidden, 0)

    @pl.when((t == 0) | (t == last))
    def _():
        for n in range(MICRO * 4):
            target, source, dest, copy = entry_copy(n)
            wait_sent(t, target, copy)

    spread_done(own_f, 0)
    spread_done(own_b, 1)

    @pl.when(t < last)
    def _():
        scatter_done(line_send_f, rs_send_f, 0)
        pass_on().wait_send()

    scatter_done(line_send_b, rs_send_b, 1)

    @pl.when(t > 0)
    def _():
        pass_above().wait_send()

    pltpu.make_async_copy(final_recv, final_recv, final_sem.at[0]).wait()
    mine = lax.broadcasted_iota(jnp.int32, (ROWS, 1), 0) == lax.rem(r, ROWS)
    for j in range(4):
        rows = jnp.where(mine, final_recv[j].astype(F32), 0.0)
        grad_out[:, j * QUART : (j + 1) * QUART] = jnp.sum(rows, axis=0, keepdims=True).astype(BF)

    @pl.when(t == 0)
    def _():
        def one(n, carry):
            target, copy = final_copy(n)
            wait_sent(own_i, target, copy)
            return carry

        lax.fori_loop(0, ROWS, one, 0)


def body(tokens, cotangent, wiring, lengths, in_proj, out_proj, section_gain):
    vmem = pl.BlockSpec(memory_space=pltpu.VMEM)
    smem = pl.BlockSpec(memory_space=pltpu.SMEM)
    hbm = pl.BlockSpec(memory_space=pl.ANY)
    dma = pltpu.SemaphoreType.DMA
    normed, masked, pre_grad, act, grad = pl.pallas_call(
        kernel,
        name="relay",
        out_shape=(
            jax.ShapeDtypeStruct((CHUNKS, MICRO, ROWS, D), BF),
            jax.ShapeDtypeStruct((CHUNKS, MICRO, ROWS, D), BF),
            jax.ShapeDtypeStruct((CHUNKS, MICRO, ROWS, PIECE), BF),
            jax.ShapeDtypeStruct((CHUNKS, MICRO, ROWS, PIECE), BF),
            jax.ShapeDtypeStruct((1, D), BF),
        ),
        in_specs=[smem, smem, hbm, hbm, hbm, hbm, hbm],
        out_specs=(vmem,) * 5,
        scratch_shapes=[
            pltpu.VMEM((CHUNKS, MICRO, ROWS, D), BF),
            pltpu.VMEM((CHUNKS, MICRO, ROWS, D), BF),
            pltpu.VMEM((D, FF_DEV), BF),
            pltpu.VMEM((D, FF_DEV), BF),
            pltpu.VMEM((GROUPS, D), BF),
            pltpu.VMEM((GROUPS, D), F32),
            pltpu.VMEM((MICRO, D), BF),
            pltpu.VMEM((MICRO, 4, 1, QUART), F32),
            pltpu.VMEM((ROWS, 1, QUART), F32),
            pltpu.VMEM((CHUNKS, SLOT_ROWS, D), BF),
            pltpu.VMEM((CHUNKS, SLOT_ROWS, FF_DEV), F32),
            pltpu.VMEM((CHUNKS, SLOT_ROWS, 128), F32),
            pltpu.VMEM((CHUNKS, SLOT_ROWS, FF_DEV), BF),
            pltpu.VMEM((CHUNKS, SLOT_ROWS, FF_DEV), F32),
            pltpu.VMEM((GROUPS, CHUNKS, SLOT_ROWS, PIECE), BF),
            pltpu.VMEM((GROUPS, CHUNKS, SLOT_ROWS, PIECE), BF),
            pltpu.VMEM((GROUPS, CHUNKS, SLOT_ROWS, PIECE), BF),
            pltpu.VMEM((GROUPS, CHUNKS, SLOT_ROWS, PIECE), BF),
            pltpu.VMEM((CHUNKS, SLOT_ROWS, HALF), BF),
            pltpu.VMEM((SLOT_ROWS, HALF), BF),
            pltpu.VMEM((CHUNKS, SLOT_ROWS, HALF), BF),
            pltpu.VMEM((CHUNKS, 4, 2, ROWS, QUART), BF),
            pltpu.VMEM((CHUNKS, 4, 2, ROWS, QUART), BF),
            pltpu.VMEM((CHUNKS, 2, ROWS, QUART), BF),
            pltpu.VMEM((LINE, ROWS, QUART), BF),
            pltpu.VMEM((ROWS, QUART), BF),
            pltpu.VMEM((ROWS, QUART), BF),
            pltpu.VMEM((CHUNKS, SLOT_ROWS, HALF), BF),
            pltpu.VMEM((CHUNKS, SLOT_ROWS, HALF), BF),
            pltpu.VMEM((CHUNKS, 4, 2, ROWS, QUART), BF),
            pltpu.VMEM((CHUNKS, 4, 2, ROWS, QUART), BF),
            pltpu.VMEM((CHUNKS, 2, ROWS, QUART), BF),
            pltpu.VMEM((2, LINE, ROWS, QUART), BF),
            pltpu.VMEM((ROWS, QUART), BF),
            pltpu.VMEM((ROWS, QUART), BF),
            pltpu.VMEM((ROWS, QUART), BF),
            pltpu.VMEM((4, ROWS, QUART), BF),
            dma((4,)),
            pltpu.SemaphoreType.REGULAR,
            dma((1,)),
            dma((1,)),
            dma((CHUNKS,)),
            dma((CHUNKS,)),
            dma((CHUNKS,)),
            dma((CHUNKS,)),
            dma((1,)),
            dma((CHUNKS,)),
            dma((CHUNKS,)),
            dma((1,)),
            dma((2, CHUNKS)),
            dma((2,)),
            dma((3,)),
            dma((2,)),
            dma((2,)),
            dma((2,)),
            dma((2,)),
            dma((2, GROUPS)),
            dma((2, GROUPS)),
            dma((1,)),
            dma((1,)),
        ],
        compiler_params=pltpu.CompilerParams(
            collective_id=0, has_side_effects=True, vmem_limit_bytes=63 * 1024 * 1024
        ),
    )(wiring.transpose(0, 2, 1), lengths, tokens.reshape(MICRO, D), cotangent.reshape(MICRO, D), in_proj[0, 0], out_proj[0, 0], section_gain[0])
    rows = CHUNKS * MICRO * ROWS
    contract = (((0,), (0,)), ((), ()))
    in_grad = lax.dot_general(
        normed.reshape(rows, D), pre_grad.reshape(rows, PIECE), contract, preferred_element_type=F32
    )
    out_grad = lax.dot_general(
        masked.reshape(rows, D), act.reshape(rows, PIECE), contract, preferred_element_type=F32
    )
    return grad[None], in_grad.astype(BF)[None], out_grad.astype(BF)[None]


def solution(mesh):
    in_specs = (
        P(None, "replica", None),
        P(None, "replica", None),
        P(),
        P(),
        P("section", "replica", None, None),
        P("section", "replica", None, None),
        P("section", None, None),
    )
    out_specs = (
        P("section", "replica", None),
        P("section", None, "replica"),
        P("section", None, "replica"),
    )
    return jax.shard_map(body, mesh=mesh, in_specs=in_specs, out_specs=out_specs, check_vma=False)
```

time: 379 us -> 210 us (0.55)
  the two profiles are of different devices: /device:TPU:229 before, /device:TPU:1 now
where the time goes in v2:
time: 210 us; the launch traced here: 206 us
  Pallas kernels  201 us (96%)
  matrix products  4.05 us (2%)
    pallas_call x1, Pallas kernels, body(): pl.pallas_call(kernel, name='relay', out_shape=(jax.ShapeDtypeStruct((CHU...  201 us

profile of v2, /device:TPU:1, one launch (start us, length us, event | category | flops | bytes accessed | tf_op | source)
XLA Modules:
  0.0 206.1 jit_solution(3447601652054248394)
XLA Ops:
  0.6 200.8 %relay.1 = (bf16[4,4,16,2560]{3,2,1,0:T(8,128)(2,1)}, bf16[4,4,16,2560]{3,2,1,0:T(8,128)(2,1)}, bf16[4,4,16,160]{3,2,1,0:T(8,128)(2,1)}, bf16[4,4,16,160]{3,2,1,0:T(8,128)(2,1)}, bf16[1,2560]{1,0:T(2,128)(2,1)}) custom-call(s32[4,1,4]{2,1,0:T(1,128)} %bitcast.39, s32[4]{0:T(128)} %lengths.1, bf16[4,2560]{1,0:T(4,128)(2,1)} %bitcast.35, ...), custom_call_target="tpu_custom_call" | custom-call | tf_op jit(solution)/shard_map/relay/pallas_call | solution.py:580
  201.4 0.0 copy-start
  201.4 0.0 copy-start.1
  201.4 2.7 %fusion.3 = bf16[1,2560,160]{1,2,0:T(8,128)(2,1)} fusion(bf16[4,4,16,2560]{3,2,1,0:T(8,128)(2,1)} %get-tuple-element.9, bf16[4,4,16,160]{3,2,1,0:T(8,128)(2,1)} %get-tuple-element.10), kind=kOutput, calls=%fused_computation.5 | convolution fusion | flops 210124800 | bytes 2211840 | tf_op jit(solution)/shard_map/dot_general | solution.py:660
  204.2 0.0 copy-done
  204.2 0.0 copy-done.1
  204.2 0.0 copy-start.2
  204.2 1.3 fusion.2
  205.5 0.0 copy-done.2
  205.5 0.6 copy.14
Async XLA Ops:
  201.4 2.8 %copy-start = (bf16[4,4,16,2560]{3,2,1,0:T(8,128)(2,1)S(1)}, bf16[4,4,16,2560]{3,2,1,0:T(8,128)(2,1)}, u32[]{:S(2)}) copy-start(bf16[4,4,16,2560]{3,2,1,0:T(8,128)(2,1)} %get-tuple-element.11) | copy-start | bytes 3932164
  201.4 2.8 %copy-start.1 = (bf16[4,4,16,160]{3,2,1,0:T(8,128)(2,1)S(1)}, bf16[4,4,16,160]{3,2,1,0:T(8,128)(2,1)}, u32[]{:S(2)}) copy-start(bf16[4,4,16,160]{3,2,1,0:T(8,128)(2,1)} %get-tuple-element.12) | copy-start | bytes 245764
  204.2 1.3 copy-start.2

commit v3 on v2

--- a/solution.py
+++ b/solution.py
@@ -18,6 +18,10 @@
 PIECE = FF_DEV // GROUPS
 CHIPS = 32
 LINE = 8
+SPREAD_ORDER = sorted(
+    ((dz, dy) for dz in range(8) for dy in range(4)),
+    key=lambda shift: -(min(shift[0], 8 - shift[0]) + min(shift[1], 4 - shift[1])),
+)
 
 gelu_coeff = 0.7978845608028654
 gelu_cubic = 0.044715
@@ -44,10 +48,11 @@
     x_buf, u_buf, w_in, w_out, gain_rows, gains, entry_rows, entry_send, entry_recv,
     h_buf, pre_buf, inv_buf, act_buf, back_buf, pg_stage, act_stage, pg_all, act_all,
     merge_send_f, merge_own, merge_recv_f, line_send_f, line_recv_f, rs_send_f, rs_recv_f, own_f, held_recv,
-    merge_send_b, merge_recv_b, line_send_b, line_recv_b, rs_send_b, rs_recv_b, own_b, above_recv, final_own, final_recv,
+    merge_send_b, merge_recv_b, line_send_b, line_recv_b, rs_send_b, rs_recv_b, own_b, above_recv,
+    final_above, final_own, final_recv,
     load_sem, go_sem, entry_sem, entry_send_sem, x_sem, x_core_sem, u_sem, u_core_sem, core_send_sem,
     merge_sem_f, merge_sem_b, merge_send_sem, line_sem, line_send_sem, rs_sem, rs_send_sem, ag_send_sem,
-    pass_sem, pass_send_sem, grads_sem, grads_send_sem, final_sem, final_send_sem,
+    pass_sem, pass_send_sem, above_sem, above_send_sem, grads_sem, grads_send_sem, final_sem, final_send_sem,
 ):
     t = lax.axis_index("section")
     r = lax.axis_index("replica")
@@ -162,13 +167,22 @@
     for shift in (1, planes - 1):
         pl.semaphore_signal(barrier, inc=1, **to(lax.rem(t + shift, planes), r))
 
-    @pl.when(t > 0)
-    def _():
-        final_z = [owner_z(lax.div(r, ROWS), oc) for oc in range(2)]
-        for j in range(4):
-            oy = 2 * (j % 2) + lax.rem(t, 2)
-            target = (final_z[j // 2] + 4 * lax.div(t, 2)) * 8 + oy * 2 + j // 2
-            pl.semaphore_signal(barrier, inc=1, **to(0, target))
+    is_final = (lax.rem(y, 2) == lax.rem(t, 2)) & (lax.rem(z, 2) == lax.div(t, 2))
+    final_k = lax.div(z, 2)
+    final_j = 2 * core + lax.div(y, 2)
+
+    @pl.when(t == 2)
+    def _():
+        def tell_first(n, carry):
+            pl.semaphore_signal(barrier, inc=1, **to(0, n * 8 + y * 2 + other))
+            return carry
+
+        lax.fori_loop(0, LINE, tell_first, 0)
+
+    @pl.when((t > 0) & is_final)
+    def _():
+        holder = (4 * lax.div(t, 2) + owner_z(final_k, core)) * 8 + y * 2 + core
+        pl.semaphore_signal(barrier, inc=1, **to(0, holder))
 
     @pl.when(ends)
     def _():
@@ -180,7 +194,7 @@
 
     gain_load.wait()
     gains[...] = gain_rows[...].astype(F32)
-    pl.semaphore_wait(barrier, replicas - 1 + 2 * LINE + 2 + jnp.where((t == 0) & (own_i > 0), ROWS, 0))
+    pl.semaphore_wait(barrier, replicas - 1 + 2 * LINE + 2 + jnp.where(t == 0, LINE + jnp.where(own_i > 0, 1, 0), 0))
 
     @pl.when(ends)
     def _():
@@ -269,31 +283,40 @@
             )
             for jj in range(2):
                 line_send[k, 2 * jj + i % 2, i // 2] = merged[:, jj * QUART : (jj + 1) * QUART]
-        for there in range(4):
+        for dy in (2, 1, 3, 0):
+            there = lax.rem(y + dy, 4)
             pltpu.make_async_remote_copy(
                 line_send.at[k, there], line_recv.at[k, y], line_send_sem.at[way], line_sem.at[way, k],
                 **to(t, line_base + 2 * there),
             ).start()
 
-    def relay(k, section, line_recv, rs_send, rs_recv, way, slot):
+    def relay(k, target, line_recv, rs_send, rs_recv, way, slot):
         pltpu.make_async_copy(line_recv.at[k], line_recv.at[k], line_sem.at[way, k]).wait()
-        base = owner_z(k, other) * 8 + y * 2 + other
         for n in range(2):
+            section, there = target(k, n)
             pieces = [line_recv[k, e, n].astype(F32) for e in range(4)]
             rs_send[k, n] = ((pieces[0] + pieces[1]) + (pieces[2] + pieces[3])).astype(BF)
             pltpu.make_async_remote_copy(
                 rs_send.at[k, n], rs_recv.at[z], rs_send_sem.at[way], rs_sem.at[slot],
-                **to(section, base + 32 * n),
+                **to(section, there),
             ).start()
 
-    def relay_turn(k, section, line_recv, rs_send, rs_recv, way, slot):
+    def forward_target(k, n):
+        return t + 1, (owner_z(k, other) + 4 * n) * 8 + y * 2 + other
+
+    def backward_target(k, n):
+        section = jnp.where(t == 0, 2 * n + lax.rem(y, 2), t - 1)
+        line = jnp.where(t == 0, 2 * k + n, owner_z(k, other) + 4 * n)
+        return section, line * 8 + y * 2 + other
+
+    def relay_turn(k, target, line_recv, rs_send, rs_recv, way, slot):
         @pl.when(k > 0)
         def _():
-            relay(k - 1, section, line_recv, rs_send, rs_recv, way, slot)
+            relay(k - 1, target, line_recv, rs_send, rs_recv, way, slot)
 
         @pl.when(k == CHUNKS - 1)
         def _():
-            relay(k, section, line_recv, rs_send, rs_recv, way, slot)
+            relay(k, target, line_recv, rs_send, rs_recv, way, slot)
 
     def scatter_done(line_send, rs_send, way):
         pltpu.make_async_copy(line_send, line_send, line_send_sem.at[way]).wait()
@@ -303,16 +326,15 @@
         position = k * ROWS + lax.broadcasted_iota(jnp.int32, (ROWS, 1), 0)
         return position < length
 
-    spread_z = [lax.rem(z + dz, 8) * 8 + other for dz in (4, 3, 5, 2, 6, 1, 7, 0)]
-    spread_y = [lax.rem(y + dy, 4) * 2 for dy in (2, 1, 3, 0)]
+    spread_z = [lax.rem(z + dz, 8) * 8 + other for dz in range(8)]
+    spread_y = [lax.rem(y + dy, 4) * 2 for dy in range(4)]
 
     def spread(source, buf, sem, way):
-        for base in spread_z:
-            for add in spread_y:
-                pltpu.make_async_remote_copy(
-                    source, buf.at[own_k, own_i, :, own_cols], ag_send_sem.at[way], sem.at[own_k],
-                    **to(t, base + add),
-                ).start()
+        for dz, dy in SPREAD_ORDER:
+            pltpu.make_async_remote_copy(
+                source, buf.at[own_k, own_i, :, own_cols], ag_send_sem.at[way], sem.at[own_k],
+                **to(t, spread_z[dz] + spread_y[dy]),
+            ).start()
 
     def spread_done(source, way):
         def one(n, carry):
@@ -329,6 +351,12 @@
     def pass_on():
         return pass_copy(own_f, held_recv, t + 1, 0)
 
+    def final_above_copy():
+        target = (2 * own_k + lax.div(own_i, 2)) * 8 + y * 2 + core
+        return target, pltpu.make_async_remote_copy(
+            own_b, final_above, above_send_sem.at[0], above_sem.at[0], **to(own_i, target)
+        )
+
     def pass_above():
         return pass_copy(own_b, above_recv, t - 1, 1)
 
@@ -379,6 +407,11 @@
         @pl.when(t > 0)
         def _():
             pass_above().start()
+
+        @pl.when(t == 0)
+        def _():
+            target, copy = final_above_copy()
+            start_or_keep(own_i, target, copy, own_b, final_above, above_sem.at[0])
 
     def gather_normed(k, carry):
         for i in range(MICRO):
@@ -438,7 +471,7 @@
                 return lax.dot_general(act, w_out[rows, :], NT, preferred_element_type=F32).astype(BF)
 
             scatter(k, half, merge_send_f, merge_recv_f, line_send_f, line_recv_f, merge_sem_f, 0)
-            relay_turn(k, t + 1, line_recv_f, rs_send_f, rs_recv_f, 0, 0)
+            relay_turn(k, forward_target, line_recv_f, rs_send_f, rs_recv_f, 0, 0)
             return carry
 
         lax.fori_loop(0, CHUNKS, step, 0)
@@ -446,7 +479,6 @@
         send_act()
         lax.fori_loop(0, CHUNKS, gather_normed, 0)
 
-    back_section = jnp.maximum(t - 1, 0)
     back_slot = jnp.where(t == 0, 1, 0)
 
     def back(k, carry):
@@ -483,7 +515,7 @@
         scatter(k, half, merge_send_b, merge_recv_b, line_send_b, line_recv_b, merge_sem_b, 1)
         for n in range(GROUPS):
             pg_stage[n, k] = pre_grad[:, n * PIECE : (n + 1) * PIECE]
-        relay_turn(k, back_section, line_recv_b, rs_send_b, rs_recv_b.at[back_slot], 1, 1 + back_slot)
+        relay_turn(k, backward_target, line_recv_b, rs_send_b, rs_recv_b.at[back_slot], 1, 1 + back_slot)
         return carry
 
     lax.fori_loop(0, CHUNKS, back, 0)
@@ -505,18 +537,18 @@
     act_all[g] = act_stage[g]
 
     def final_copy(n):
-        target = own_k * ROWS + n
+        target = final_k * ROWS + n
         return target, pltpu.make_async_remote_copy(
-            final_own, final_recv.at[own_j], final_send_sem.at[0], final_sem.at[0], **to(own_i, target)
+            final_own, final_recv.at[final_j], final_send_sem.at[0], final_sem.at[0], **to(t, target)
         )
 
-    @pl.when(t == 0)
-    def _():
-        final_own[...] = combined(own_b[...], rs_recv_b.at[1], 2)
+    def send_final():
+        pltpu.make_async_copy(final_above, final_above, above_sem.at[0]).wait()
+        final_own[...] = combined(final_above[...], rs_recv_b.at[1], 2)
 
         def one(n, carry):
             target, copy = final_copy(n)
-            start_or_keep(own_i, target, copy, final_own, final_recv.at[own_j], final_sem.at[0])
+            start_or_keep(t, target, copy, final_own, final_recv.at[final_j], final_sem.at[0])
             return carry
 
         lax.fori_loop(0, ROWS, one, 0)
@@ -534,7 +566,17 @@
                 out[k, i] = choose(routes[i] * CAP + slots[i], pieces)
         return carry
 
-    lax.fori_loop(0, CHUNKS, gather_hidden, 0)
+    @pl.when(t > 0)
+    def _():
+        lax.fori_loop(0, CHUNKS, gather_hidden, 0)
+
+    @pl.when(is_final)
+    def _():
+        send_final()
+
+    @pl.when(t == 0)
+    def _():
+        lax.fori_loop(0, CHUNKS, gather_hidden, 0)
 
     @pl.when((t == 0) | (t == last))
     def _():
@@ -564,9 +606,14 @@
 
     @pl.when(t == 0)
     def _():
+        target, copy = final_above_copy()
+        wait_sent(own_i, target, copy)
+
+    @pl.when(is_final)
+    def _():
         def one(n, carry):
             target, copy = final_copy(n)
-            wait_sent(own_i, target, copy)
+            wait_sent(t, target, copy)
             return carry
 
         lax.fori_loop(0, ROWS, one, 0)
@@ -626,6 +673,7 @@
             pltpu.VMEM((ROWS, QUART), BF),
             pltpu.VMEM((ROWS, QUART), BF),
             pltpu.VMEM((ROWS, QUART), BF),
+            pltpu.VMEM((ROWS, QUART), BF),
             pltpu.VMEM((4, ROWS, QUART), BF),
             dma((4,)),
             pltpu.SemaphoreType.REGULAR,
@@ -646,6 +694,8 @@
             dma((2,)),
             dma((2,)),
             dma((2,)),
+            dma((1,)),
+            dma((1,)),
             dma((2, GROUPS)),
             dma((2, GROUPS)),
             dma((1,)),
@@ -655,15 +705,35 @@
             collective_id=0, has_side_effects=True, vmem_limit_bytes=63 * 1024 * 1024
         ),
     )(wiring.transpose(0, 2, 1), lengths, tokens.reshape(MICRO, D), cotangent.reshape(MICRO, D), in_proj[0, 0], out_proj[0, 0], section_gain[0])
+    column_block = pl.BlockSpec((CHUNKS, MICRO, ROWS, QUART), lambda n: (0, 0, 0, n))
+    hidden_block = pl.BlockSpec((CHUNKS, MICRO, ROWS, PIECE), lambda n: (0, 0, 0, 0))
+    out_block = pl.BlockSpec((PIECE, QUART), lambda n: (0, n))
+    row_block = pl.BlockSpec((1, QUART), lambda n: (0, n))
+    in_grad, out_grad, grad = pl.pallas_call(
+        weight_kernel,
+        name="weights",
+        grid=(4,),
+        out_shape=(
+            jax.ShapeDtypeStruct((PIECE, D), BF),
+            jax.ShapeDtypeStruct((PIECE, D), BF),
+            jax.ShapeDtypeStruct((1, D), BF),
+        ),
+        in_specs=[column_block, hidden_block, column_block, hidden_block, row_block],
+        out_specs=(out_block, out_block, row_block),
+        compiler_params=pltpu.CompilerParams(vmem_limit_bytes=63 * 1024 * 1024),
+    )(normed, pre_grad, masked, act, grad)
+    return grad[None], in_grad.T[None], out_grad.T[None]
+
+
+def weight_kernel(normed, pre_grad, masked, act, row, in_out, out_out, row_out):
     rows = CHUNKS * MICRO * ROWS
-    contract = (((0,), (0,)), ((), ()))
-    in_grad = lax.dot_general(
-        normed.reshape(rows, D), pre_grad.reshape(rows, PIECE), contract, preferred_element_type=F32
-    )
-    out_grad = lax.dot_general(
-        masked.reshape(rows, D), act.reshape(rows, PIECE), contract, preferred_element_type=F32
-    )
-    return grad[None], in_grad.astype(BF)[None], out_grad.astype(BF)[None]
+    for hidden, features, out in ((pre_grad, normed, in_out), (act, masked, out_out)):
+        value = lax.dot_general(
+            hidden[...].reshape(rows, PIECE), features[...].reshape(rows, QUART),
+            (((0,), (0,)), ((), ())), preferred_element_type=F32,
+        )
+        out[...] = value.astype(BF)
+    row_out[...] = row[...]
 
 
 def solution(mesh):

time: 210 us -> 204 us (0.971); the launches traced: 206 us -> 203 us
  matrix products: 4.05 us -> 0 us
    pallas_call x0 -> x1, Pallas kernels: none -> 4.46 us  [body(): pl.pallas_call(weight_kernel, name='weights', grid=(4,), out_shape=(jax.S...]
    dot_general x2 -> x0, matrix products: 4.05 us -> none  [the longest x1 2.74 us: body(): lax.dot_general(normed.reshape(rows, D), pre_grad.reshape(rows, PIECE), c...]
    pallas_call x1, Pallas kernels: 201 us -> 198 us  [body(): pl.pallas_call(kernel, name='relay', out_shape=(jax.ShapeDtypeStruct((CHU...]
where the time goes in v3:
time: 204 us; the launch traced here: 203 us
  Pallas kernels  203 us (100%)
    pallas_call x1, Pallas kernels, body(): pl.pallas_call(kernel, name='relay', out_shape=(jax.ShapeDtypeStruct((CHU...  198 us
    pallas_call x1, Pallas kernels, body(): pl.pallas_call(weight_kernel, name='weights', grid=(4,), out_shape=(jax.S...  4.46 us

profile of v3, /device:TPU:1, one launch (start us, length us, event | category | flops | bytes accessed | tf_op | source)
XLA Modules:
  0.0 203.5 jit_solution(8747574783207408742)
XLA Ops:
  0.6 198.4 %relay.1 = (bf16[4,4,16,2560]{3,2,1,0:T(8,128)(2,1)}, bf16[4,4,16,2560]{3,2,1,0:T(8,128)(2,1)}, bf16[4,4,16,160]{3,2,1,0:T(8,128)(2,1)}, bf16[4,4,16,160]{3,2,1,0:T(8,128)(2,1)}, bf16[1,2560]{1,0:T(2,128)(2,1)}) custom-call(s32[4,1,4]{2,1,0:T(1,128)} %bitcast.20, s32[4]{0:T(128)} %lengths.1, bf16[4,2560]{1,0:T(4,128)(2,1)} %bitcast.17, ...), custom_call_target="tpu_custom_call" | custom-call | tf_op jit(solution)/shard_map/relay/pallas_call | solution.py:627
  199.0 4.5 %weights.1 = (bf16[160,2560]{1,0:T(8,128)(2,1)}, bf16[160,2560]{1,0:T(8,128)(2,1)}, bf16[1,2560]{1,0:T(2,128)(2,1)}) custom-call(bf16[4,4,16,2560]{3,2,1,0:T(8,128)(2,1)} %get-tuple-element.11.normed, bf16[4,4,16,160]{3,2,1,0:T(8,128)(2,1)} %get-tuple-element.12.pre_grad, bf16[4,4,16,2560]{3,2,1,0:T(8,128)(2,1)} %get-tuple-element.13.masked, ...), custom_call_target="tpu_custom_call" | custom-call | tf_op jit(solution)/shard_map/weights/pallas_call | solution.py:712

commit v4 on v3

--- a/solution.py
+++ b/solution.py
@@ -705,14 +705,14 @@
             collective_id=0, has_side_effects=True, vmem_limit_bytes=63 * 1024 * 1024
         ),
     )(wiring.transpose(0, 2, 1), lengths, tokens.reshape(MICRO, D), cotangent.reshape(MICRO, D), in_proj[0, 0], out_proj[0, 0], section_gain[0])
-    column_block = pl.BlockSpec((CHUNKS, MICRO, ROWS, QUART), lambda n: (0, 0, 0, n))
+    column_block = pl.BlockSpec((CHUNKS, MICRO, ROWS, HALF), lambda n: (0, 0, 0, n))
     hidden_block = pl.BlockSpec((CHUNKS, MICRO, ROWS, PIECE), lambda n: (0, 0, 0, 0))
-    out_block = pl.BlockSpec((PIECE, QUART), lambda n: (0, n))
-    row_block = pl.BlockSpec((1, QUART), lambda n: (0, n))
+    out_block = pl.BlockSpec((PIECE, HALF), lambda n: (0, n))
+    row_block = pl.BlockSpec((1, HALF), lambda n: (0, n))
     in_grad, out_grad, grad = pl.pallas_call(
         weight_kernel,
         name="weights",
-        grid=(4,),
+        grid=(2,),
         out_shape=(
             jax.ShapeDtypeStruct((PIECE, D), BF),
             jax.ShapeDtypeStruct((PIECE, D), BF),
@@ -729,7 +729,7 @@
     rows = CHUNKS * MICRO * ROWS
     for hidden, features, out in ((pre_grad, normed, in_out), (act, masked, out_out)):
         value = lax.dot_general(
-            hidden[...].reshape(rows, PIECE), features[...].reshape(rows, QUART),
+            hidden[...].reshape(rows, PIECE), features[...].reshape(rows, HALF),
             (((0,), (0,)), ((), ())), preferred_element_type=F32,
         )
         out[...] = value.astype(BF)

time: 204 us -> 202 us (level)
  no operation moved by 1% of the time
where the time goes in v4:
time: 202 us
  Pallas kernels  202 us (100%)
    pallas_call x1, Pallas kernels, body(): pl.pallas_call(kernel, name='relay', out_shape=(jax.ShapeDtypeStruct((CHU...  198 us

profile of v4, /device:TPU:1, one launch (start us, length us, event | category | flops | bytes accessed | tf_op | source)
XLA Modules:
  0.0 202.2 jit_solution(7239863276314437234)
XLA Ops:
  0.6 198.4 %relay.1 = (bf16[4,4,16,2560]{3,2,1,0:T(8,128)(2,1)}, bf16[4,4,16,2560]{3,2,1,0:T(8,128)(2,1)}, bf16[4,4,16,160]{3,2,1,0:T(8,128)(2,1)}, bf16[4,4,16,160]{3,2,1,0:T(8,128)(2,1)}, bf16[1,2560]{1,0:T(2,128)(2,1)}) custom-call(s32[4,1,4]{2,1,0:T(1,128)} %bitcast.20, s32[4]{0:T(128)} %lengths.1, bf16[4,2560]{1,0:T(4,128)(2,1)} %bitcast.17, ...), custom_call_target="tpu_custom_call" | custom-call | tf_op jit(solution)/shard_map/relay/pallas_call | solution.py:627
  199.0 3.2 %weights.1 = (bf16[160,2560]{1,0:T(8,128)(2,1)}, bf16[160,2560]{1,0:T(8,128)(2,1)}, bf16[1,2560]{1,0:T(2,128)(2,1)}) custom-call(bf16[4,4,16,2560]{3,2,1,0:T(8,128)(2,1)} %get-tuple-element.11.normed, bf16[4,4,16,160]{3,2,1,0:T(8,128)(2,1)} %get-tuple-element.12.pre_grad, bf16[4,4,16,2560]{3,2,1,0:T(8,128)(2,1)} %get-tuple-element.13.masked, ...), custom_call_target="tpu_custom_call" | custom-call | tf_op jit(solution)/shard_map/weights/pallas_call | solution.py:712

commit v5 on v4

--- a/solution.py
+++ b/solution.py
@@ -720,18 +720,22 @@
         ),
         in_specs=[column_block, hidden_block, column_block, hidden_block, row_block],
         out_specs=(out_block, out_block, row_block),
+        scratch_shapes=[pltpu.VMEM((2, PIECE, CHUNKS * MICRO * ROWS), BF)],
         compiler_params=pltpu.CompilerParams(vmem_limit_bytes=63 * 1024 * 1024),
     )(normed, pre_grad, masked, act, grad)
     return grad[None], in_grad.T[None], out_grad.T[None]
 
 
-def weight_kernel(normed, pre_grad, masked, act, row, in_out, out_out, row_out):
+def weight_kernel(normed, pre_grad, masked, act, row, in_out, out_out, row_out, turned):
     rows = CHUNKS * MICRO * ROWS
-    for hidden, features, out in ((pre_grad, normed, in_out), (act, masked, out_out)):
-        value = lax.dot_general(
-            hidden[...].reshape(rows, PIECE), features[...].reshape(rows, HALF),
-            (((0,), (0,)), ((), ())), preferred_element_type=F32,
-        )
+
+    @pl.when(pl.program_id(0) == 0)
+    def _():
+        for n, hidden in enumerate((pre_grad, act)):
+            turned[n] = hidden[...].reshape(rows, PIECE).astype(F32).T.astype(BF)
+
+    for n, (features, out) in enumerate(((normed, in_out), (masked, out_out))):
+        value = jnp.dot(turned[n], features[...].reshape(rows, HALF), preferred_element_type=F32)
         out[...] = value.astype(BF)
     row_out[...] = row[...]
 

time: 202 us -> 202 us (level)
  no operation moved by 1% of the time
where the time goes in v5:
time: 202 us
  Pallas kernels  202 us (100%)
    pallas_call x1, Pallas kernels, body(): pl.pallas_call(kernel, name='relay', out_shape=(jax.ShapeDtypeStruct((CHU...  198 us

profile of v5, /device:TPU:1, one launch (start us, length us, event | category | flops | bytes accessed | tf_op | source)
XLA Modules:
  0.0 202.3 jit_solution(6596508660788354566)
XLA Ops:
  0.6 198.4 %relay.1 = (bf16[4,4,16,2560]{3,2,1,0:T(8,128)(2,1)}, bf16[4,4,16,2560]{3,2,1,0:T(8,128)(2,1)}, bf16[4,4,16,160]{3,2,1,0:T(8,128)(2,1)}, bf16[4,4,16,160]{3,2,1,0:T(8,128)(2,1)}, bf16[1,2560]{1,0:T(2,128)(2,1)}) custom-call(s32[4,1,4]{2,1,0:T(1,128)} %bitcast.20, s32[4]{0:T(128)} %lengths.1, bf16[4,2560]{1,0:T(4,128)(2,1)} %bitcast.17, ...), custom_call_target="tpu_custom_call" | custom-call | tf_op jit(solution)/shard_map/relay/pallas_call | solution.py:627
  199.0 3.3 %weights.1 = (bf16[160,2560]{1,0:T(8,128)(2,1)}, bf16[160,2560]{1,0:T(8,128)(2,1)}, bf16[1,2560]{1,0:T(2,128)(2,1)}) custom-call(bf16[4,4,16,2560]{3,2,1,0:T(8,128)(2,1)} %get-tuple-element.11.normed, bf16[4,4,16,160]{3,2,1,0:T(8,128)(2,1)} %get-tuple-element.12.pre_grad, bf16[4,4,16,2560]{3,2,1,0:T(8,128)(2,1)} %get-tuple-element.13.masked, ...), custom_call_target="tpu_custom_call" | custom-call | tf_op jit(solution)/shard_map/weights/pallas_call | solution.py:712
